TPU v7x, 32 devices: a whole 2x2x4 slice. The times are simulated.
32 devices in a mesh: dp: 8 (over z, y), fsdp: 4 (over x, core).
Axes of the slice: x: 2, y: 2, z: 4, core: 2. Of those that a mesh axis runs over, the one named last changes fastest.
Arguments:
- images: bfloat16 [32, 32, 128, 256], P(('dp', 'fsdp')), may hold values from -6 to 6
- targets: bfloat16 [32, 32, 128, 256], P(('dp', 'fsdp')), may hold values from -6 to 6
- pixel_mask: int32 [32, 32, 128], P(('dp', 'fsdp')), may hold values from 0 to 1, as said below
- encfirst: bfloat16 [2304, 64], P('dp', 'fsdp'), may hold values from -0.125 to 0.125
- encsecond: bfloat16 [576, 64], P('dp', 'fsdp'), may hold values from -0.25 to 0.25
- encthird: bfloat16 [576, 64], P('dp', 'fsdp'), may hold values from -0.25 to 0.25
- encfourth: bfloat16 [64, 256], P('dp', 'fsdp'), may hold values from -96 to 96
- encbiasa: bfloat16 [64], P('dp'), may hold values from -1 to 1
- encbiasb: bfloat16 [64], P('dp'), may hold values from -1 to 1
- encbiasc: bfloat16 [64], P('dp'), may hold values from -1 to 1
- encbiasd: bfloat16 [256], P('dp'), may hold values from -1 to 1
- decfirst: bfloat16 [256, 64], P('dp', 'fsdp'), may hold values from -0.375 to 0.375
- decsecond: bfloat16 [576, 64], P('dp', 'fsdp'), may hold values from -0.25 to 0.25
- decthird: bfloat16 [576, 64], P('dp', 'fsdp'), may hold values from -0.25 to 0.25
- decfourth: bfloat16 [576, 256], P('dp', 'fsdp'), may hold values from -24 to 24
- decbiasa: bfloat16 [64], P('dp'), may hold values from -1 to 1
- decbiasb: bfloat16 [64], P('dp'), may hold values from -1 to 1
- decbiasc: bfloat16 [64], P('dp'), may hold values from -1 to 1
- decbiasd: bfloat16 [256], P('dp'), may hold values from -1 to 1
Outputs:
- decoded: bfloat16 [32, 32, 128, 256], P(('dp', 'fsdp'))
- images_grad: bfloat16 [32, 32, 128, 256], P(('dp', 'fsdp'))
- image_loss: float32 [32], P(('dp', 'fsdp'))
- encfirst_grad: float32 [2304, 64], P('dp', 'fsdp')
- encsecond_grad: float32 [576, 64], P('dp', 'fsdp')
- encthird_grad: float32 [576, 64], P('dp', 'fsdp')
- encfourth_grad: float32 [64, 256], P('dp', 'fsdp')
- encbiasa_grad: float32 [64], P('dp')
- encbiasb_grad: float32 [64], P('dp')
- encbiasc_grad: float32 [64], P('dp')
- encbiasd_grad: float32 [256], P('dp')
- decfirst_grad: float32 [256, 64], P('dp', 'fsdp')
- decsecond_grad: float32 [576, 64], P('dp', 'fsdp')
- decthird_grad: float32 [576, 64], P('dp', 'fsdp')
- decfourth_grad: float32 [576, 256], P('dp', 'fsdp')
- decbiasa_grad: float32 [64], P('dp')
- decbiasb_grad: float32 [64], P('dp')
- decbiasc_grad: float32 [64], P('dp')
- decbiasd_grad: float32 [256], P('dp')
Inputs may be any that keep to these rules, and one draw needn't show every extreme that they name: `pixel_mask`: each image's mask is 1 on the rectangle of its first rows and first columns, at least 16 rows and 64 columns, and 0 elsewhere; at least its last row and its last column are 0.
All inputs are finite; a program needn't handle non-finite values.
Results may differ from a plain program's by a relative error of at most 0.0066.
Values may be sent and summed in bfloat16 or wider, within the bound.
A program may use at most 128 MiB of HBM per device.

v0:
```python
import functools
import jax
import jax.numpy as jnp
from jax import lax
from jax.experimental import pallas as pl
from jax.experimental.pallas import tpu as pltpu
from jax.sharding import PartitionSpec as P

F32, BF16 = jnp.float32, jnp.bfloat16
MESH = pl.DeviceIdType.MESH


def dot(a, b):
    return jnp.dot(a, b, preferred_element_type=F32)


def dot_t(a, b):
    return lax.dot_general(a, b, (((1,), (1,)), ((), ())), preferred_element_type=F32)


def dot_p(a, b):
    return lax.dot_general(a, b, (((0,), (0,)), ((), ())), preferred_element_type=F32)


def loop(count, body, unroll):
    if unroll >= count:
        for c in range(count):
            body(c)
    else:
        def step(k, _):
            for u in range(unroll):
                body(k * unroll + u)
            return 0
        lax.fori_loop(0, count // unroll, step, 0)


def masks():
    lane = lax.broadcasted_iota(jnp.int32, (1, 1, 8, 128), 3)
    row = lax.broadcasted_iota(jnp.int32, (1, 1, 8, 128), 2)
    return lane < 64, row


def shifted(x):
    n = x.shape[0]
    _, row = masks()
    x4 = x.reshape(n, 8, 8, 128)
    nxt = jnp.where(row == 7, 0.0, pltpu.roll(x4[:, :1], 7, 2))
    prv = jnp.where(row == 0, 0.0, pltpu.roll(x4[:, 7:], 1, 2))
    up = jnp.concatenate([x4[:, 1:], nxt], axis=1)
    dn = jnp.concatenate([prv, x4[:, :7]], axis=1)
    return up, dn


def beside(x):
    lo, _ = masks()
    up, dn = shifted(x)
    return jnp.where(lo, up, dn).reshape(x.shape)


def folded(x):
    lo, _ = masks()
    up, dn = shifted(x)
    return jnp.where(lo, dn, up).reshape(x.shape)


def silu_parts(v):
    h = 0.5 * v
    u = 1.0 + jnp.tanh(h)
    act = h * u
    w = 0.5 * u
    return act, w + act * (1.0 - w)


def part_sum(x):
    return x.reshape(-1, 8, x.shape[-1]).sum(axis=0)


def put_pair(ref, idx, x):
    n = x.shape[0]
    ref[pl.ds(idx, n), :, 0:128] = x.astype(BF16)
    ref[pl.ds(idx, n), :, 128:256] = beside(x).astype(BF16)


def quad_rows(ref, r0, n, d):
    return jnp.concatenate([ref[2 * (r0 + k) + d] for k in range(n)], axis=0)


def split_rows(acc, n):
    a = acc.reshape(n, 1, 64, 256)
    return jnp.concatenate([a[..., :128], a[..., 128:]], axis=1).reshape(2 * n, 64, 128)


def stack_in(k):
    z = jnp.zeros_like(k[0])
    rows = ((k[1], k[2]), (k[0], k[1]), (z, k[0]), (k[2], z))
    return jnp.concatenate([jnp.concatenate(r, axis=1) for r in rows], axis=0)


def stack_out(k):
    z = jnp.zeros_like(k[0])
    rows = ((k[1], k[2], z, k[0]), (k[0], k[1], k[2], z))
    return jnp.concatenate([jnp.concatenate(r, axis=1) for r in rows], axis=0)


TAPS = ("ef", "es", "et", "df", "ds", "dt")
ROWS = dict(ef=2304, es=576, et=576, df=256, ds=576, dt=576, do=576)


def places(dp):
    enc, dec, at = {}, {}, 0
    for k in ("ef", "es", "et"):
        enc[k] = (at, ROWS[k] // dp)
        at += ROWS[k] // dp
    enc["extra"] = (at, 64)
    wide = at + 64
    at = 0
    for k in ("df", "ds", "dt"):
        dec[k] = (at, ROWS[k] // dp)
        at += ROWS[k] // dp
    for k in range(4):
        dec[k] = (at, ROWS["do"] // dp)
        at += ROWS["do"] // dp
    wide = max(wide, at)
    return enc, dec, wide + (-wide % 128)


def extra_block(eo, enc_row, dec_row):
    r = eo.shape[0]
    fill = lambda v: jnp.concatenate([v, jnp.zeros((1, 64 - v.shape[1]), F32)], axis=1)
    parts = [eo] + ([jnp.zeros((8 - r, 64), F32)] if r < 8 else [])
    return jnp.concatenate(parts + [fill(enc_row), fill(dec_row), jnp.zeros((6, 64), F32)], axis=0)


def lanes_to(parts, wide):
    at = sum(p.shape[1] for p in parts)
    if at < wide:
        parts = parts + [jnp.zeros((parts[0].shape[0], wide - at), parts[0].dtype)]
    return jnp.concatenate(parts, axis=1)


def where_am_i():
    a, b = lax.axis_index("dp"), lax.axis_index("fsdp")
    return a // 2, lax.rem(a, 2), b // 2, lax.rem(b, 2)


def device(z, y, x, c):
    return (z * 2 + y, x * 2 + c)


def far_copy(src, dst, send, recv, to):
    cp = pltpu.make_async_remote_copy(
        src_ref=src, dst_ref=dst, send_sem=send, recv_sem=recv, device_id=to, device_id_type=MESH)
    cp.start()
    return cp


def wait_all(copies):
    for cp in copies:
        cp.wait()


class Gather:
    def __init__(self, me, buf, send, recv):
        self.me, self.buf, self.send, self.recv = me, buf, send, recv
        self.nz = buf.shape[0]
        self.h = self.nz // 2

    def copy(self, view, k, to):
        return far_copy(view, view, self.send.at[k], self.recv.at[k], device(*to))

    def along_z(self):
        z, y, x, c = self.me
        mine = self.buf.at[z, y, x, c]
        self.fly = [self.copy(mine, 3 + k, (lax.rem(z + k, self.nz), y, x, c)) for k in range(1, self.nz)]

    def square_one(self):
        z, y, x, c = self.me
        wait_all(self.fly)
        lo, hi = pl.ds(0, self.h), pl.ds(self.h, self.nz - self.h)
        self.fly = [self.copy(self.buf.at[lo, y, x, c], 0, (z, 1 - y, x, c)),
                    self.copy(self.buf.at[hi, y, x, c], 1, (z, y, 1 - x, c))]

    def square_two(self):
        z, y, x, c = self.me
        wait_all(self.fly)
        lo, hi = pl.ds(0, self.h), pl.ds(self.h, self.nz - self.h)
        self.fly = [self.copy(self.buf.at[lo, :, x, c], 2, (z, y, 1 - x, c)),
                    self.copy(self.buf.at[hi, y, :, c], 3, (z, 1 - y, x, c))]

    def cores(self):
        z, y, x, c = self.me
        wait_all(self.fly)
        self.fly = [self.copy(self.buf.at[:, :, :, c], self.nz + 3, (z, y, x, 1 - c))]

    def finish(self):
        wait_all(self.fly)


def add16(p, q):
    return (p.astype(F32) + q.astype(F32)).astype(BF16)


class Scatter:
    def __init__(self, me, part, bufs, send, recv):
        self.me, self.part, self.send, self.recv = me, part, send, recv
        self.in1, self.s1, self.in2a, self.in2b, self.s2a, self.s2b, self.in3, self.s3, self.in4 = bufs
        self.nz = part.shape[0]
        self.h = self.nz // 2

    def copy(self, src, dst, k, to):
        return far_copy(src, dst, self.send.at[k], self.recv.at[k], device(*to))

    def cores(self):
        z, y, x, c = self.me
        self.fly = [self.copy(self.part.at[:, :, :, 1 - c], self.in1, 0, (z, y, x, 1 - c))]

    def square_one(self):
        z, y, x, c = self.me
        h, n = self.h, self.nz - self.h
        wait_all(self.fly)
        for k in range(self.nz):
            self.s1[k] = add16(self.part[k, :, :, c], self.in1[k])
        self.fly = [self.copy(self.s1.at[pl.ds(0, h), :, 1 - x], self.in2a, 1, (z, y, 1 - x, c)),
                    self.copy(self.s1.at[pl.ds(h, n), 1 - y], self.in2b, 2, (z, 1 - y, x, c))]

    def square_two(self):
        z, y, x, c = self.me
        h, n = self.h, self.nz - self.h
        wait_all(self.fly)
        for k in range(h):
            self.s2a[k] = add16(self.s1[k, :, x], self.in2a[k])
        for k in range(n):
            self.s2b[k] = add16(self.s1[h + k, y], self.in2b[k])
        self.fly = [self.copy(self.s2a.at[:, 1 - y], self.in3.at[pl.ds(0, h)], 3, (z, 1 - y, x, c)),
                    self.copy(self.s2b.at[:, 1 - x], self.in3.at[pl.ds(h, n)], 4, (z, y, 1 - x, c))]

    def along_z(self):
        z, y, x, c = self.me
        h, n = self.h, self.nz - self.h
        wait_all(self.fly)
        for k in range(h):
            self.s3[k] = add16(self.s2a[k, y], self.in3[k])
        for k in range(n):
            self.s3[h + k] = add16(self.s2b[k, x], self.in3[h + k])
        self.fly = []
        for k in range(1, self.nz):
            other = lax.rem(z + k, self.nz)
            self.fly.append(self.copy(self.s3.at[other], self.in4.at[k], 4 + k, (other, y, x, c)))

    def finish(self, out):
        z = self.me[0]
        wait_all(self.fly)
        total = self.s3[z].astype(F32)
        for k in range(1, self.nz):
            total = total + self.in4[k].astype(F32)
        out[...] = total


def main_kernel(U, *refs):
    (images_h, targets_h, mask_h, ef_h, es_h, et_h, eo_h, df_h, ds_h, dt_h, do_h, *rest) = refs
    biases_h, rest = rest[:8], rest[8:]
    (decoded_h, images_grad_h, loss, tot_e, tot_d,
     images, targets, mask, ef_s, es_s, et_s, eo_s, df_s, ds_s, dt_s, do_s, *rest) = rest
    biases_s, rest = rest[:8], rest[8:]
    (decoded, images_grad, src, act0, sl_src, z1, z2, a3, y1, y2, y3, s1, s2, s3, t1, t2, t3,
     mid, sl_mid, d0, g4, h4, zg, zh, stage,
     w_ef, w_es, w_et, v_es, v_et, w_ds, w_dt, v_ds, v_dt, w_do, w_eo, w_df, bias, bacc, eacc,
     whole_e, whole_d, part_e, part_d, *rest) = rest
    bufs_e, bufs_d, rest = rest[:9], rest[9:18], rest[18:]
    (shard_sem, image_sem, io_sem, ge_send, ge_recv, gd_send, gd_recv, se_send, se_recv, sd_send, sd_recv) = rest

    nz = whole_e.shape[0]
    dp = nz * 2
    enc_at, dec_at, wide = places(dp)
    me = where_am_i()
    z, y, x, c = me

    def near(src, dst, sem):
        cp = pltpu.make_async_copy(src, dst, sem)
        cp.start()
        return cp
    shards_h = (ef_h, es_h, et_h, eo_h, df_h, ds_h, dt_h, do_h, *biases_h)
    shards_s = (ef_s, es_s, et_s, eo_s, df_s, ds_s, dt_s, do_s, *biases_s)
    shard_copies = [near(p, q, shard_sem.at[k]) for k, (p, q) in enumerate(zip(shards_h, shards_s))]
    image_copies = [near(images_h.at[pl.ds(8 * k, 8)], images.at[pl.ds(8 * k, 8)], image_sem.at[k]) for k in range(4)]
    target_copy = near(targets_h, targets, io_sem.at[0])
    mask_copy = near(mask_h, mask, io_sem.at[1])

    barrier = pltpu.get_barrier_semaphore()
    others = [device(lax.rem(z + k, nz), y, x, c) for k in range(1, nz)]
    others += [device(z, 1 - y, x, c), device(z, y, 1 - x, c), device(z, y, x, 1 - c)]
    for d in others:
        pl.semaphore_signal(barrier, inc=1, device_id=d, device_id_type=MESH)
    wait_all(shard_copies)
    enc_row = jnp.concatenate([b[...].astype(F32) for b in biases_s[:4]], axis=1)
    dec_row = jnp.concatenate([b[...].astype(F32) for b in biases_s[4:]], axis=1)
    extra = extra_block(eo_s[...].astype(F32), enc_row, dec_row).astype(BF16)
    whole_e[z, y, x, c] = lanes_to([ef_s[...], es_s[...], et_s[...], extra], wide)
    whole_d[z, y, x, c] = lanes_to([df_s[...], ds_s[...], dt_s[...]] + [do_s[16 * k:16 * k + 16] for k in range(4)], wide)
    pl.semaphore_wait(barrier, len(others))
    ge = Gather(me, whole_e, ge_send, ge_recv)
    gd = Gather(me, whole_d, gd_send, gd_recv)
    ge.along_z()
    gd.along_z()

    for ref in (act0, g4, z1, z2, y1, y2, y3, zg, zh):
        ref[0] = jnp.zeros(ref.shape[1:], ref.dtype)
        ref[33] = jnp.zeros(ref.shape[1:], ref.dtype)
    bacc[...] = jnp.zeros_like(bacc)
    eacc[...] = jnp.zeros_like(eacc)

    def across(whole, place):
        at, n = place
        return jnp.concatenate([
            jnp.concatenate([whole[a // 2, a % 2, b // 2, b % 2, :, at:at + n] for b in range(4)], axis=0)
            for a in range(dp)], axis=1)

    def tap(k, i, n):
        return [k[:, (3 * i + j) * n:(3 * i + j + 1) * n] for j in range(3)]

    def quad_weights(k, w_ref, v_ref):
        w_ref[0, 128:256, :] = jnp.zeros((128, 256), BF16)
        w_ref[3, 0:128, :] = jnp.zeros((128, 256), BF16)
        v_ref[0, :, 128:256] = jnp.zeros((256, 128), BF16)
        v_ref[3, :, 0:128] = jnp.zeros((256, 128), BF16)
        for i in range(3):
            t = tap(k, i, 64)
            f = stack_out(t)
            w_ref[i, 0:128, :] = f
            w_ref[i + 1, 128:256, :] = f
            b = stack_in(t)
            v_ref[2 - i, :, 0:128] = b
            v_ref[3 - i, :, 128:256] = b

    def two(k):
        z = jnp.zeros_like(k)
        return jnp.concatenate([jnp.concatenate([k, z], axis=1), jnp.concatenate([z, k], axis=1)], axis=0)

    r_eo = 64 // dp
    b_at = [(0, 64 // dp), (64 // dp, 64 // dp), (128 // dp, 64 // dp), (192 // dp, 256 // dp)]

    def encoder_weights():
        k = across(whole_e, enc_at["ef"])
        for i in range(3):
            w_ef[i] = stack_in(tap(k, i, 256))
        quad_weights(across(whole_e, enc_at["es"]), w_es, v_es)
        quad_weights(across(whole_e, enc_at["et"]), w_et, v_et)
        at, n = enc_at["extra"]
        blocks = [[whole_e[a // 2, a % 2, b // 2, b % 2, :, at:at + n].astype(F32) for b in range(4)] for a in range(dp)]
        w_eo[...] = two(jnp.concatenate([
            jnp.concatenate([blk[0:r_eo] for blk in blocks[a]], axis=1) for a in range(dp)], axis=0).astype(BF16))
        for row in range(2):
            for k, (at, size) in enumerate(b_at):
                v = jnp.concatenate([blocks[a][0][8 + row:9 + row, at:at + size] for a in range(dp)], axis=1)
                v = jnp.concatenate([v, v], axis=1)
                if k < 3:
                    bias[3 * row + k, :, 0:128] = v
                else:
                    bias[6 + row] = v * (1.0 / 64.0)

    def decoder_weights():
        w_df[...] = two(across(whole_d, dec_at["df"]))
        quad_weights(across(whole_d, dec_at["ds"]), w_ds, v_ds)
        quad_weights(across(whole_d, dec_at["dt"]), w_dt, v_dt)
        quarter = [across(whole_d, dec_at[k]) for k in range(4)]
        k = jnp.concatenate([quarter[k][16 * b:16 * b + 16] for b in range(4) for k in range(4)], axis=0)
        for i in range(3):
            w_do[i] = stack_out(tap(k, i, 64))

    def to_pairs(v, slot):
        stage[slot, 0] = v[:, :128]
        stage[slot, 1] = v[:, 128:]
        return [jnp.concatenate([stage[slot, h, pl.ds(2 * t + e, 8, stride=16), :] for t in range(8)], axis=0)
                for e in range(2) for h in range(2)]

    def to_natural(v, slot):
        for e in range(2):
            for h in range(2):
                for t in range(8):
                    stage[slot, h, pl.ds(2 * t + e, 8, stride=16), :] = v[8 * t:8 * t + 8, e * 256 + h * 128:e * 256 + h * 128 + 128]
        return stage[slot, 0], stage[slot, 1]

    def body_b(p):
        v = images[p].astype(F32)
        slot = p % 4 if isinstance(p, int) else lax.rem(p, 4)
        parts = to_pairs(v, slot)
        for q, x in enumerate(parts):
            ln = slice(q * 128, q * 128 + 128)
            act, slope = silu_parts(x)
            src[p, :, ln] = x.astype(BF16)
            act0[p + 1, :, ln] = act.astype(BF16)
            sl_src[p, :, ln] = slope
    def rows_b(k):
        image_copies[k].wait()
        loop(8, lambda r: body_b(8 * k + r), U['B'])
    rows_b(0)
    ge.square_one()
    rows_b(1)
    ge.square_two()
    rows_b(2)
    ge.cores()
    gd.square_one()
    rows_b(3)
    ge.finish()
    encoder_weights()

    def hidden(pre, b, slope_ref, row):
        act, slope = silu_parts(pre + bias[b, :, 0:128])
        slope_ref[pl.ds(row, pre.shape[0])] = slope
        return act

    n = U['nC']
    def body(c):
        p = c * n
        acc = 0.0
        for i in range(3):
            acc = acc + dot_t(act0[pl.ds(p + i, n)].reshape(n * 64, 512), w_ef[i])
        acc = acc.reshape(n, 64, 256)
        pre = acc[..., :128] + folded(acc[..., 128:])
        put_pair(z1, p + 1, hidden(pre, 0, s1, p))
    loop(32 // n, body, U['C'])

    def quad_conv(zin, w, b, slope_ref, zout, n, unroll, pair=True):
        def body(c):
            acc = 0.0
            for d in range(4):
                acc = acc + dot_t(quad_rows(zin, c * n, n, d), w[d])
            act = hidden(split_rows(acc, n), b, slope_ref, c * 2 * n)
            if pair:
                put_pair(zout, c * 2 * n + 1, act)
            else:
                zout[pl.ds(c * 2 * n, 2 * n)] = act.astype(BF16)
        loop(16 // n, body, unroll)

    gd.square_two()
    quad_conv(z1, w_es, 1, s2, z2, U['nQ'], U['Q'])
    gd.cores()
    quad_conv(z2, w_et, 2, s3, a3, U['nQ'], U['Q'], pair=False)

    gd.finish()
    decoder_weights()

    n = U['nF']
    def body(c):
        p = c * n
        br = dot(a3[pl.ds(p, n)].reshape(n * 64, 128), w_eo[...])
        m = src[pl.ds(p, n)].astype(F32).reshape(n * 64, 512) + (br * (1.0 / 64.0) + bias[6])
        act, slope = silu_parts(m)
        mid[pl.ds(p, n)] = m.reshape(n, 64, 512)
        sl_mid[pl.ds(p, n)] = slope.reshape(n, 64, 512)
        act = act.astype(BF16)
        d0[pl.ds(p, n)] = act.reshape(n, 64, 512)
        pre = dot_t(act, w_df[...]).reshape(n, 64, 128)
        put_pair(y1, p + 1, hidden(pre, 3, t1, p))
    loop(32 // n, body, U['F'])

    quad_conv(y1, w_ds, 4, t2, y2, U['nQ'], U['Q'])
    quad_conv(y2, w_dt, 5, t3, y3, U['nQ'], U['Q'])

    mask_copy.wait()
    target_copy.wait()
    mk = mask[...].astype(F32)
    tall = jnp.sum(mk[:, 0:1])
    broad = jnp.sum(mk[0:1, :])
    sub = lax.broadcasted_iota(jnp.int32, (64, 128), 0)
    column = lax.rem(sub, 8) * 16 + 2 * (sub // 8)
    wi = broad.astype(jnp.int32)
    hi = tall.astype(jnp.int32)
    col_mask = [jnp.where(column + e < wi, 1.0, 0.0) for e in range(2)]
    n = U['nJ']
    def body(c):
        p = c * n
        acc = 0.0
        for i in range(3):
            acc = acc + dot_t(y3[pl.ds(p + i, n)].reshape(n * 64, 256), w_do[i])
        acc = acc.reshape(n, 64, 512)
        for r in range(n):
            m = mid[p + r]
            res = m + (acc[r] * (1.0 / 64.0) + bias[7])
            slot = r % 2
            a, b = to_natural(res, 2 + slot)
            decoded[p + r, :, 0:128] = a.astype(BF16)
            decoded[p + r, :, 128:256] = b.astype(BF16)
            t = to_pairs(targets[p + r].astype(F32), slot)
            row_on = jnp.where(p + r < hi, 1.0, 0.0)
            for q in range(4):
                ln = slice(q * 128, q * 128 + 128)
                diff = res[:, ln] - t[q]
                g = diff * (col_mask[q // 2] * row_on)
                mid[p + r, :, ln] = g
                eacc[...] += part_sum(g * diff)
                g = g * (1.0 / 64.0)
                g4[p + r + 1, :, ln] = g.astype(BF16)
                bacc[7, :, ln] += part_sum(g)
    loop(32 // n, body, U['J'])
    decoded_copy = near(decoded, decoded_h, io_sem.at[2])
    loss[0] = 0.5 * jnp.sum(eacc[...]) / (tall * broad * 256.0)

    def back(x, slope_ref, row, b):
        g = x * slope_ref[pl.ds(row, x.shape[0])]
        bacc[b, :, 0:128] += part_sum(g)
        return g

    n = U['nC']
    def body(c):
        p = c * n
        acc = 0.0
        for i in range(3):
            acc = acc + dot(g4[pl.ds(p + i, n)].reshape(n * 64, 512), w_do[2 - i])
        acc = acc.reshape(n, 64, 256)
        x = acc[..., :128] + folded(acc[..., 128:])
        put_pair(zg, p + 1, back(x, t3, p, 5))
    loop(32 // n, body, U['K'])

    M = [3, 0, 1, 2]

    gv = g4[pl.ds(1, 32)].reshape(2048, 512)
    cols = []
    for i in range(3):
        t = dot_p(gv, y3[pl.ds(i, 32)].reshape(2048, 256))
        for j in range(3):
            a, b = M[j] * 64, M[j + 1] * 64
            cols.append(t[0:256, a:a + 64] + t[256:512, b:b + 64])
    k_do = jnp.concatenate(cols, axis=1).astype(BF16)
    for a in range(dp):
        n = 576 // dp
        v = k_do[:, n * a:n * a + n]
        for b in range(4):
            for k in range(4):
                at = dec_at[k][0]
                r = 64 * b + 16 * k
                part_d[a // 2, a % 2, b // 2, b % 2, :, at:at + n] = v[r:r + 16]

    def deal(part, place, k):
        at, n = place
        k = k.astype(BF16)
        for a in range(dp):
            v = k[:, n * a:n * a + n]
            for b in range(4):
                part[a // 2, a % 2, b // 2, b % 2, :, at:at + n] = v[16 * b:16 * b + 16]

    def quad_wgrad(z, g_ref, part, place):
        gq = jnp.concatenate([
            jnp.concatenate([g_ref[2 * r + 1, :, 0:128] for r in range(16)], axis=0),
            jnp.concatenate([g_ref[2 * r + 2, :, 0:128] for r in range(16)], axis=0)], axis=1)
        t = [dot_p(gq, quad_rows(z, 0, 16, d)) for d in range(4)]
        cols = []
        for i in range(3):
            s = t[i][0:128] + t[i + 1][128:256]
            for j in range(3):
                a, b = M[j] * 64, M[j + 1] * 64
                cols.append(s[0:64, a:a + 64] + s[64:128, b:b + 64])
        deal(part, place, jnp.concatenate(cols, axis=1))

    def quad_back(zin, v, slope_ref, b, zout, n, unroll):
        def body(c):
            acc = 0.0
            for d in range(4):
                acc = acc + dot(quad_rows(zin, c * n, n, d), v[d])
            put_pair(zout, c * 2 * n + 1, back(split_rows(acc, n), slope_ref, c * 2 * n, b))
        loop(16 // n, body, unroll)

    quad_back(zg, v_dt, t2, 4, zh, U['nQ'], U['Q'])
    quad_wgrad(y2, zg, part_d, dec_at["dt"])
    quad_back(zh, v_ds, t1, 3, zg, U['nQ'], U['Q'])
    quad_wgrad(y1, zh, part_d, dec_at["ds"])

    t = dot_p(zg[pl.ds(1, 32), :, 0:128].reshape(2048, 128), d0[...].reshape(2048, 512))
    deal(part_d, dec_at["df"], t[0:64, 0:256] + t[64:128, 256:512])
    sd = Scatter(me, part_d, bufs_d, sd_send, sd_recv)
    sd.cores()

    n = U['nF']
    def body(c):
        p = c * n
        bk = dot(zg[pl.ds(p + 1, n), :, 0:128].reshape(n * 64, 128), w_df[...])
        gm = mid[pl.ds(p, n)].reshape(n * 64, 512) + sl_mid[pl.ds(p, n)].reshape(n * 64, 512) * bk
        mid[pl.ds(p, n)] = gm.reshape(n, 64, 512)
        g = gm * (1.0 / 64.0)
        bacc[6] += part_sum(g)
        g = g.astype(BF16)
        h4[pl.ds(p, n)] = g.reshape(n, 64, 512)
        x = dot_t(g, w_eo[...]).reshape(n, 64, 128)
        put_pair(zh, p + 1, back(x, s3, p, 2))
    loop(32 // n, body, U['F'])

    sd.square_one()

    t = dot_p(a3[...].reshape(2048, 128), h4[...].reshape(2048, 512))
    k_eo = t[0:64, 0:256] + t[64:128, 256:512]

    quad_back(zh, v_et, s2, 1, zg, U['nQ'], U['Q'])
    sd.square_two()
    quad_wgrad(z2, zh, part_e, enc_at["et"])
    sd.along_z()
    quad_back(zg, v_es, s1, 0, zh, U['nQ'], U['Q'])
    quad_wgrad(z1, zg, part_e, enc_at["es"])

    gv = zh[pl.ds(1, 32)].reshape(2048, 256)
    cols = []
    for i in range(3):
        t = dot_p(gv, act0[pl.ds(i, 32)].reshape(2048, 512))
        cols.append(t[64:128, 0:256] + t[128:192, 256:512])
        cols.append(t[0:64, 0:256] + t[64:128, 256:512])
        cols.append(t[192:256, 0:256] + t[0:64, 256:512])
    deal(part_e, enc_at["ef"], jnp.concatenate(cols, axis=1))
    sd.finish(tot_d)

    sums = []
    for n in range(8):
        v = jnp.sum(bacc[n], axis=0, keepdims=True)
        sums.append(v[:, 0:256] + v[:, 256:512] if n >= 6 else v[:, 0:64] + v[:, 64:128])
    at = enc_at["extra"][0]
    for a in range(dp):
        rows = []
        for group in ((0, 1, 2, 6), (3, 4, 5, 7)):
            rows.append(jnp.concatenate([sums[k][:, a * n:a * n + n] for k, (_, n) in zip(group, b_at)], axis=1))
        for b in range(4):
            extra = extra_block(k_eo[a * r_eo:a * r_eo + r_eo, 64 * b:64 * b + 64], *rows)
            part_e[a // 2, a % 2, b // 2, b % 2, :, at:at + 64] = extra.astype(BF16)
    se = Scatter(me, part_e, bufs_e, se_send, se_recv)
    se.cores()

    n = U['nJ']
    def body_q(c):
        p = c * n
        acc = 0.0
        for i in range(3):
            acc = acc + dot(zh[pl.ds(p + i, n)].reshape(n * 64, 256), w_ef[2 - i])
        acc = acc.reshape(n, 64, 512)
        for r in range(n):
            g = mid[p + r] + sl_src[p + r] * acc[r]
            a, b = to_natural(g, r % 4)
            images_grad[p + r, :, 0:128] = a.astype(BF16)
            images_grad[p + r, :, 128:256] = b.astype(BF16)
    grad_copies = []

    def rows_q(k):
        loop(8 // n, lambda r: body_q(k * (8 // n) + r), U['Qr'])
        grad_copies.append(near(images_grad.at[pl.ds(8 * k, 8)], images_grad_h.at[pl.ds(8 * k, 8)], image_sem.at[k]))
    rows_q(0)
    se.square_one()
    rows_q(1)
    se.square_two()
    rows_q(2)
    se.along_z()
    rows_q(3)
    se.finish(tot_e)
    decoded_copy.wait()
    wait_all(grad_copies)


def last_kernel(decoded_i, images_grad_i, loss_i, tot_e, tot_d, decoded, images_grad, loss, *refs):
    g_ef, g_es, g_et, g_eo, g_df, g_ds, g_dt, g_do = refs[:8]
    biases, hold, sem = refs[8:16], refs[16], refs[17]
    dp = 64 // g_eo.shape[0]
    pairs = [(p, q, n * 4 + k, pl.ds(8 * k, 8)) for k in range(4) for n, (p, q) in enumerate(((decoded_i, decoded), (images_grad_i, images_grad)))]
    ins = [pltpu.make_async_copy(p.at[rows], hold.at[k], sem.at[k]) for p, q, k, rows in pairs]
    outs = [pltpu.make_async_copy(hold.at[k], q.at[rows], sem.at[8 + k]) for p, q, k, rows in pairs]
    for cp in ins:
        cp.start()
    loss[0] = loss_i[0]
    enc_at, dec_at, wide = places(dp)
    e, d = tot_e[...], tot_d[...]
    for k, ref in (("ef", g_ef), ("es", g_es), ("et", g_et)):
        at, n = enc_at[k]
        ref[...] = e[:, at:at + n]
    for k, ref in (("df", g_df), ("ds", g_ds), ("dt", g_dt)):
        at, n = dec_at[k]
        ref[...] = d[:, at:at + n]
    for k in range(4):
        at, n = dec_at[k]
        g_do[16 * k:16 * k + 16] = d[:, at:at + n]
    at = enc_at["extra"][0]
    g_eo[...] = e[0:64 // dp, at:at + 64]
    for row in range(2):
        off = at
        for k in range(4):
            n = (64, 64, 64, 256)[k] // dp
            biases[4 * row + k][...] = e[8 + row:9 + row, off:off + n]
            off += n
    for p, q in zip(ins, outs):
        p.wait()
        q.start()
    wait_all(outs)


U = dict(B=4, nC=8, C=1, K=1, nQ=8, Q=1, nF=4, F=1, nJ=4, J=1, Qr=1)


def per_device(images, targets, pixel_mask, ef, es, et, eo, eba, ebb, ebc, ebd, df, ds, dt, do, dba, dbb, dbc, dbd):
    dp = lax.axis_size("dp")
    nz = dp // 2
    h = nz // 2
    wide = places(dp)[2]
    vm = pl.BlockSpec(memory_space=pltpu.VMEM)
    far = pl.BlockSpec(memory_space=pl.ANY)
    smem = pl.BlockSpec(memory_space=pltpu.SMEM)
    sem = pltpu.SemaphoreType.DMA
    V = lambda shape, dt: pltpu.VMEM(shape, dt)
    S = jax.ShapeDtypeStruct
    args = [images[0], targets[0], pixel_mask[0], ef.T, es.T, et.T, eo, df.T, ds.T, dt.T, do.T]
    args += [b.reshape(1, -1) for b in (eba, ebb, ebc, ebd, dba, dbb, dbc, dbd)]
    comm = [V((nz, 2, 2, 16, wide), BF16), V((nz, 2, 2, 16, wide), BF16), V((h, 2, 16, wide), BF16), V((nz - h, 2, 16, wide), BF16),
            V((h, 2, 16, wide), BF16), V((nz - h, 2, 16, wide), BF16), V((nz, 16, wide), BF16), V((nz, 16, wide), BF16),
            V((nz, 16, wide), BF16)]
    big = S((32, 128, 256), BF16)
    tot = S((16, wide), F32)
    decoded, images_grad, loss, tot_e, tot_d = pl.pallas_call(
        functools.partial(main_kernel, U),
        out_shape=[big, big, S((1,), F32), tot, tot],
        in_specs=[far] * 19, out_specs=[far, far, smem, vm, vm],
        scratch_shapes=[V(a.shape, a.dtype) for a in args] + [
            V((32, 128, 256), BF16), V((32, 128, 256), BF16),
            V((32, 64, 512), BF16), V((34, 64, 512), BF16), V((32, 64, 512), F32),
            V((34, 64, 256), BF16), V((34, 64, 256), BF16), V((32, 64, 128), BF16),
            V((34, 64, 256), BF16), V((34, 64, 256), BF16), V((34, 64, 256), BF16)] + [V((32, 64, 128), F32)] * 6 + [
            V((32, 64, 512), F32), V((32, 64, 512), F32), V((32, 64, 512), BF16),
            V((34, 64, 512), BF16), V((32, 64, 512), BF16), V((34, 64, 256), BF16), V((34, 64, 256), BF16),
            V((4, 2, 128, 128), F32),
            V((3, 256, 512), BF16)] + [V((4, 256, 256), BF16)] * 8 + [
            V((3, 512, 256), BF16), V((128, 512), BF16), V((128, 512), BF16),
            V((8, 1, 512), F32), V((8, 8, 512), F32), V((8, 128), F32)]
        + [V((nz, 2, 2, 2, 16, wide), BF16)] * 4 + comm * 2
        + [sem((16,)), sem((4,)), sem((3,))] + [sem((nz + 4,))] * 8,
        compiler_params=pltpu.CompilerParams(collective_id=0, has_side_effects=True, vmem_limit_bytes=63 * 2**20),
    )(*args)
    f = lambda *s: S(s, F32)
    outs = pl.pallas_call(
        last_kernel,
        out_shape=[big, big, S((1,), F32), f(16, 2304 // dp), f(16, 576 // dp), f(16, 576 // dp), f(64 // dp, 64), f(16, 256 // dp),
                   f(16, 576 // dp), f(16, 576 // dp), f(64, 576 // dp)] + [f(1, s // dp) for s in (64, 64, 64, 256) * 2],
        in_specs=[far, far, smem, vm, vm], out_specs=[far, far, smem] + [vm] * 16, scratch_shapes=[V((8, 8, 128, 256), BF16), sem((16,))],
        compiler_params=pltpu.CompilerParams(vmem_limit_bytes=60 * 2**20),
    )(decoded, images_grad, loss, tot_e, tot_d)
    decoded, images_grad, loss, g_ef, g_es, g_et, g_eo, g_df, g_ds, g_dt, g_do = outs[:11]
    bs = [b.reshape(-1) for b in outs[11:]]
    return (decoded[None], images_grad[None], loss, g_ef.T, g_es.T, g_et.T, g_eo, *bs[:4],
            g_df.T, g_ds.T, g_dt.T, g_do.T, *bs[4:])


def solution(mesh):
    img, w, b = P(("dp", "fsdp"), None, None, None), P("dp", "fsdp"), P("dp")
    placed = (img, img, P(("dp", "fsdp"), None, None)) + (w,) * 4 + (b,) * 4 + (w,) * 4 + (b,) * 4
    return jax.shard_map(
        per_device, mesh=mesh, in_specs=placed,
        out_specs=(img, img, P(("dp", "fsdp"))) + (w,) * 4 + (b,) * 4 + (w,) * 4 + (b,) * 4,
        check_vma=False)
```

profile of v0, /device:TPU:0, one launch (start us, length us, event | category | flops | bytes accessed | tf_op | source)
XLA Modules:
  0.0 80.2 jit_solution(12443265995959513301)
XLA Ops:
  0.7 73.7 %shard_map.330 = (bf16[32,128,256]{2,1,0:T(8,128)(2,1)}, bf16[32,128,256]{2,1,0:T(8,128)(2,1)}, f32[1]{0:T(128)}, f32[16,512]{1,0:T(8,128)}, f32[16,512]{1,0:T(8,128)}) custom-call(bf16[32,128,256]{2,1,0:T(8,128)(2,1)} %bitcast.35, bf16[32,128,256]{2,1,0:T(8,128)(2,1)} %bitcast.36, s32[32,128]{1,0:T(8,128)} %bitcast.37, bf16[16,288]{1,0:T(8,128)(2,1)} %bitcast.39, ...), custom_call_target="tpu_custom_call" | custom-call | tf_op jit(solution)/shard_map/pallas_call | solution.py:709
  74.4 5.6 %shard_map.331 = (bf16[32,128,256]{2,1,0:T(8,128)(2,1)}, bf16[32,128,256]{2,1,0:T(8,128)(2,1)}, f32[1]{0:T(128)}, f32[16,288]{1,0:T(8,128)}, f32[16,72]{1,0:T(8,...) custom-call(bf16[32,128,256]{2,1,0:T(8,128)(2,1)} %get-tuple-element, ...), custom_call_target="tpu_custom_call" | custom-call | tf_op jit(solution)/shard_map/pallas_call | solution.py:729
where the time goes:
time: 80.5 us; the launch traced here: 80.2 us
  Pallas kernels  79.4 us (99%)
  between operations  0.83 us (1%)
    pallas_call x1, Pallas kernels, per_device(): pl.pallas_call(functools.partial(main_kernel, U), out_shape=[big, big, S(...  73.7 us
    pallas_call x1, Pallas kernels, per_device(): pl.pallas_call(last_kernel, out_shape=[big, big, S((1,), F32), f(16, 2304...  5.64 us

commit v1 on v0

v1 whole, which is shorter than its diff:
```python
import functools
import jax
import jax.numpy as jnp
from jax import lax
from jax.experimental import pallas as pl
from jax.experimental.pallas import tpu as pltpu
from jax.sharding import PartitionSpec as P

F32, BF16 = jnp.float32, jnp.bfloat16
MESH = pl.DeviceIdType.MESH


def dot(a, b):
    return jnp.dot(a, b, preferred_element_type=F32)


def dot_t(a, b):
    return lax.dot_general(a, b, (((1,), (1,)), ((), ())), preferred_element_type=F32)


def dot_p(a, b):
    return lax.dot_general(a, b, (((0,), (0,)), ((), ())), preferred_element_type=F32)


def loop(count, body, unroll):
    if unroll >= count:
        for c in range(count):
            body(c)
    else:
        def step(k, _):
            for u in range(unroll):
                body(k * unroll + u)
            return 0
        lax.fori_loop(0, count // unroll, step, 0)


def masks():
    lane = lax.broadcasted_iota(jnp.int32, (1, 1, 8, 128), 3)
    row = lax.broadcasted_iota(jnp.int32, (1, 1, 8, 128), 2)
    return lane < 64, row


def shifted(x):
    n = x.shape[0]
    _, row = masks()
    x4 = x.reshape(n, 8, 8, 128)
    nxt = jnp.where(row == 7, 0.0, pltpu.roll(x4[:, :1], 7, 2))
    prv = jnp.where(row == 0, 0.0, pltpu.roll(x4[:, 7:], 1, 2))
    up = jnp.concatenate([x4[:, 1:], nxt], axis=1)
    dn = jnp.concatenate([prv, x4[:, :7]], axis=1)
    return up, dn


def beside(x):
    lo, _ = masks()
    up, dn = shifted(x)
    return jnp.where(lo, up, dn).reshape(x.shape)


def folded(x):
    lo, _ = masks()
    up, dn = shifted(x)
    return jnp.where(lo, dn, up).reshape(x.shape)


def silu_parts(v):
    h = 0.5 * v
    u = 1.0 + jnp.tanh(h)
    act = h * u
    w = 0.5 * u
    return act, w + act * (1.0 - w)


def part_sum(x):
    return x.reshape(-1, 8, x.shape[-1]).sum(axis=0)


def put_pair(ref, idx, x):
    ref[idx, :, 0:128] = x.astype(BF16)
    ref[idx, :, 128:256] = beside(x[None])[0].astype(BF16)


def quad_rows(ref, r0, n, d):
    return jnp.concatenate([ref[2 * (r0 + k) + d] for k in range(n)], axis=0)


def rows_of(x, n):
    return [x[64 * r:64 * r + 64] for r in range(n)]


def stack_in(k):
    z = jnp.zeros_like(k[0])
    rows = ((k[1], k[2]), (k[0], k[1]), (z, k[0]), (k[2], z))
    return jnp.concatenate([jnp.concatenate(r, axis=1) for r in rows], axis=0)


def stack_out(k):
    z = jnp.zeros_like(k[0])
    rows = ((k[1], k[2], z, k[0]), (k[0], k[1], k[2], z))
    return jnp.concatenate([jnp.concatenate(r, axis=1) for r in rows], axis=0)


TAPS = ("ef", "es", "et", "df", "ds", "dt")
ROWS = dict(ef=2304, es=576, et=576, df=256, ds=576, dt=576, do=576)


def places(dp):
    groups = ((("ef", 2304 // dp), ("es", 576 // dp), ("bias", 128 // dp)),
              (("et", 576 // dp), ("df", 256 // dp), ("eo", 64)),
              (("ds", 576 // dp), ("dt", 576 // dp)) + tuple((k, 576 // dp) for k in range(4)))
    spots, widths = {}, []
    for g, group in enumerate(groups):
        at = 0
        for name, n in group:
            spots[name] = (g, at, n)
            at += n
        widths.append(at + (-at % 128))
    return spots, widths


def bias_block(parts):
    w = parts[3].shape[1] // 2
    n = parts[0].shape[1]
    fill = lambda v: jnp.concatenate([v, jnp.zeros((1, w - n), F32)], axis=1)
    rows = [fill(parts[k]) for k in (0, 1, 2, 4, 5, 6)]
    for k in (3, 7):
        rows += [parts[k][:, :w], parts[k][:, w:]]
    return jnp.concatenate(rows + [jnp.zeros((6, w), F32)], axis=0)


def bias_rows(block, n):
    thin = [block[k:k + 1, :n] for k in range(6)]
    wide = [jnp.concatenate([block[k:k + 1], block[k + 1:k + 2]], axis=1) for k in (6, 8)]
    return thin[:3] + wide[:1] + thin[3:] + wide[1:]


def eo_block(eo):
    return jnp.concatenate([eo, jnp.zeros((16 - eo.shape[0], 64), F32)], axis=0)


def lanes_to(parts, wide):
    at = sum(p.shape[1] for p in parts)
    if at < wide:
        parts = parts + [jnp.zeros((parts[0].shape[0], wide - at), parts[0].dtype)]
    return jnp.concatenate(parts, axis=1)


def where_am_i():
    a, b = lax.axis_index("dp"), lax.axis_index("fsdp")
    return a // 2, lax.rem(a, 2), b // 2, lax.rem(b, 2)


def device(z, y, x, c):
    return (z * 2 + y, x * 2 + c)


def far_copy(src, dst, send, recv, to):
    cp = pltpu.make_async_remote_copy(
        src_ref=src, dst_ref=dst, send_sem=send, recv_sem=recv, device_id=to, device_id_type=MESH)
    cp.start()
    return cp


def wait_all(copies):
    for cp in copies:
        cp.wait()


class Gather:
    def __init__(self, me, buf, send, recv):
        self.me, self.buf, self.send, self.recv = me, buf, send, recv
        self.nz = buf.shape[0]
        self.h = self.nz // 2

    def copy(self, view, k, to):
        return far_copy(view, view, self.send.at[k], self.recv.at[k], device(*to))

    def along_z(self):
        z, y, x, c = self.me
        mine = self.buf.at[z, y, x, c]
        self.fly = [self.copy(mine, 3 + k, (lax.rem(z + k, self.nz), y, x, c)) for k in range(1, self.nz)]

    def square_one(self):
        z, y, x, c = self.me
        wait_all(self.fly)
        lo, hi = pl.ds(0, self.h), pl.ds(self.h, self.nz - self.h)
        self.fly = [self.copy(self.buf.at[lo, y, x, c], 0, (z, 1 - y, x, c)),
                    self.copy(self.buf.at[hi, y, x, c], 1, (z, y, 1 - x, c))]

    def square_two(self):
        z, y, x, c = self.me
        wait_all(self.fly)
        lo, hi = pl.ds(0, self.h), pl.ds(self.h, self.nz - self.h)
        self.fly = [self.copy(self.buf.at[lo, :, x, c], 2, (z, y, 1 - x, c)),
                    self.copy(self.buf.at[hi, y, :, c], 3, (z, 1 - y, x, c))]

    def cores(self):
        z, y, x, c = self.me
        wait_all(self.fly)
        self.fly = [self.copy(self.buf.at[:, :, :, c], self.nz + 3, (z, y, x, 1 - c))]

    def finish(self):
        wait_all(self.fly)


class DirectGather:
    def __init__(self, me, buf, send, recv):
        self.me, self.buf, self.send, self.recv = me, buf, send, recv
        self.nz = buf.shape[0]
        self.steps = chip_steps(self.nz)

    def copy(self, view, k, to):
        return far_copy(view, view, self.send.at[k], self.recv.at[k], device(*to))

    def chips(self):
        z, y, x, c = self.me
        mine = self.buf.at[z, y, x, c]
        self.fly = {}
        for k, step in reversed(list(enumerate(self.steps))):
            self.fly[k] = self.copy(mine, k, other_chip(self.me, step, self.nz))

    def cores(self):
        z, y, x, c = self.me
        self.last = []
        for dz in range(self.nz):
            wait_all([self.fly[k] for k, step in enumerate(self.steps) if step[0] == dz])
            rows = self.buf.at[lax.rem(z + self.nz - dz, self.nz), :, :, c]
            self.last.append(self.copy(rows, len(self.steps) + dz, (z, y, x, 1 - c)))

    def finish(self):
        wait_all(self.last)


class DirectScatter:
    def __init__(self, me, part, bufs, send, recv):
        self.me, self.part, self.send, self.recv = me, part, send, recv
        self.in1, self.s1, self.in2 = bufs
        self.nz = part.shape[0]
        self.steps = chip_steps(self.nz)

    def copy(self, src, dst, k, to):
        return far_copy(src, dst, self.send.at[k], self.recv.at[k], device(*to))

    def cores(self):
        z, y, x, c = self.me
        self.fly = [self.copy(self.part.at[:, :, :, 1 - c], self.in1, len(self.steps), (z, y, x, 1 - c))]

    def chips(self):
        z, y, x, c = self.me
        wait_all(self.fly)
        for k in range(self.nz):
            self.s1[k] = add16(self.part[k, :, :, c], self.in1[k])
        self.fly = []
        for k, step in reversed(list(enumerate(self.steps))):
            to = other_chip(self.me, step, self.nz)
            self.fly.append(self.copy(self.s1.at[to[0], to[1], to[2]], self.in2.at[k], k, to))

    def finish(self, out):
        z, y, x, c = self.me
        wait_all(self.fly)
        total = self.s1[z, y, x].astype(F32)
        for k in range(len(self.steps)):
            total = total + self.in2[k].astype(F32)
        out[...] = total


def chip_steps(nz):
    return [(dz, dy, dx) for dz in range(nz) for dy in range(2) for dx in range(2)][1:]


def other_chip(me, step, nz):
    z, y, x, c = me
    return (lax.rem(z + step[0], nz), lax.rem(y + step[1], 2), lax.rem(x + step[2], 2), c)


def add16(p, q):
    return (p.astype(F32) + q.astype(F32)).astype(BF16)


class Scatter:
    def __init__(self, me, part, bufs, send, recv):
        self.me, self.part, self.send, self.recv = me, part, send, recv
        self.in1, self.s1, self.in2a, self.in2b, self.s2a, self.s2b, self.in3, self.s3, self.in4 = bufs
        self.nz = part.shape[0]
        self.h = self.nz // 2

    def copy(self, src, dst, k, to):
        return far_copy(src, dst, self.send.at[k], self.recv.at[k], device(*to))

    def cores(self):
        z, y, x, c = self.me
        self.fly = [self.copy(self.part.at[:, :, :, 1 - c], self.in1, 0, (z, y, x, 1 - c))]

    def square_one(self):
        z, y, x, c = self.me
        h, n = self.h, self.nz - self.h
        wait_all(self.fly)
        for k in range(self.nz):
            self.s1[k] = add16(self.part[k, :, :, c], self.in1[k])
        self.fly = [self.copy(self.s1.at[pl.ds(0, h), :, 1 - x], self.in2a, 1, (z, y, 1 - x, c)),
                    self.copy(self.s1.at[pl.ds(h, n), 1 - y], self.in2b, 2, (z, 1 - y, x, c))]

    def square_two(self):
        z, y, x, c = self.me
        h, n = self.h, self.nz - self.h
        wait_all(self.fly)
        for k in range(h):
            self.s2a[k] = add16(self.s1[k, :, x], self.in2a[k])
        for k in range(n):
            self.s2b[k] = add16(self.s1[h + k, y], self.in2b[k])
        self.fly = [self.copy(self.s2a.at[:, 1 - y], self.in3.at[pl.ds(0, h)], 3, (z, 1 - y, x, c)),
                    self.copy(self.s2b.at[:, 1 - x], self.in3.at[pl.ds(h, n)], 4, (z, y, 1 - x, c))]

    def along_z(self):
        z, y, x, c = self.me
        h, n = self.h, self.nz - self.h
        wait_all(self.fly)
        for k in range(h):
            self.s3[k] = add16(self.s2a[k, y], self.in3[k])
        for k in range(n):
            self.s3[h + k] = add16(self.s2b[k, x], self.in3[h + k])
        self.fly = []
        for k in range(1, self.nz):
            other = lax.rem(z + k, self.nz)
            self.fly.append(self.copy(self.s3.at[other], self.in4.at[k], 4 + k, (other, y, x, c)))

    def finish(self, out):
        z = self.me[0]
        wait_all(self.fly)
        total = self.s3[z].astype(F32)
        for k in range(1, self.nz):
            total = total + self.in4[k].astype(F32)
        out[...] = total


def main_kernel(U, *refs):
    (images_h, targets_h, mask_h, ef_h, es_h, et_h, eo_h, df_h, ds_h, dt_h, do_h, *rest) = refs
    biases_h, rest = rest[:8], rest[8:]
    (decoded_h, images_grad_h, loss, tot0, tot1, tot2,
     images, targets, mask, ef_s, es_s, et_s, eo_s, df_s, ds_s, dt_s, do_s, *rest) = rest
    biases_s, rest = rest[:8], rest[8:]
    decoded, images_grad = images, targets
    (src, act0, sl_src, z1, z2, a3, y1, y2, y3, s1, s2, s3, t1, t2, t3,
     mid, sl_mid, d0, g4, h4, zg, zh, stage,
     w_ef, w_es, w_et, v_es, v_et, w_ds, w_dt, v_ds, v_dt, w_do, w_eo, w_df, bias, bacc, eacc,
     *rest) = rest
    whole, part, rest = rest[:3], rest[3:6], rest[6:]
    bufs0, bufs1, bufs2, rest = rest[:3], rest[3:12], rest[12:21], rest[21:]
    shard_sem, image_sem, io_sem, *pairs = rest

    nz = whole[0].shape[0]
    dp = nz * 2
    spots, widths = places(dp)
    me = where_am_i()
    z, y, x, c = me

    def near(src, dst, sem):
        cp = pltpu.make_async_copy(src, dst, sem)
        cp.start()
        return cp
    shards_h = (ef_h, es_h, et_h, eo_h, df_h, ds_h, dt_h, do_h, *biases_h)
    shards_s = (ef_s, es_s, et_s, eo_s, df_s, ds_s, dt_s, do_s, *biases_s)
    shard_copies = [near(p, q, shard_sem.at[k]) for k, (p, q) in enumerate(zip(shards_h, shards_s))]
    image_copies = [near(images_h.at[pl.ds(8 * k, 8)], images.at[pl.ds(8 * k, 8)], image_sem.at[k]) for k in range(4)]
    target_copy = near(targets_h, targets, io_sem.at[0])
    mask_copy = near(mask_h, mask, io_sem.at[1])

    barrier = pltpu.get_barrier_semaphore()
    others = [device(*other_chip(me, step, nz)) for step in chip_steps(nz)] + [device(z, y, x, 1 - c)]
    for d in others:
        pl.semaphore_signal(barrier, inc=1, device_id=d, device_id_type=MESH)
    g0 = DirectGather(me, whole[0], *pairs[0:2])
    g1 = Gather(me, whole[1], *pairs[2:4])
    g2 = Gather(me, whole[2], *pairs[4:6])
    wait_all(shard_copies)
    bias_part = bias_block([b[...].astype(F32) for b in biases_s]).astype(BF16)
    whole[0][z, y, x, c] = lanes_to([ef_s[...], es_s[...], bias_part], widths[0])
    pl.semaphore_wait(barrier, len(others))
    g0.chips()
    whole[1][z, y, x, c] = lanes_to([et_s[...], df_s[...], eo_block(eo_s[...].astype(F32)).astype(BF16)], widths[1])
    whole[2][z, y, x, c] = lanes_to([ds_s[...], dt_s[...]] + [do_s[16 * k:16 * k + 16] for k in range(4)], widths[2])
    g1.along_z()

    for ref in (act0, g4, z1, z2, y1, y2, y3, zg, zh):
        ref[0] = jnp.zeros(ref.shape[1:], ref.dtype)
        ref[33] = jnp.zeros(ref.shape[1:], ref.dtype)
    bacc[...] = jnp.zeros_like(bacc)
    eacc[...] = jnp.zeros_like(eacc)

    def blocks(name):
        g, at, n = spots[name]
        return [[whole[g][a // 2, a % 2, b // 2, b % 2, :, at:at + n] for b in range(4)] for a in range(dp)]

    def across(name):
        return jnp.concatenate([jnp.concatenate(col, axis=0) for col in blocks(name)], axis=1)

    def tap(k, i, n):
        return [k[:, (3 * i + j) * n:(3 * i + j + 1) * n] for j in range(3)]

    def quad_weights(k, w_ref, v_ref):
        w_ref[0, 128:256, :] = jnp.zeros((128, 256), BF16)
        w_ref[3, 0:128, :] = jnp.zeros((128, 256), BF16)
        v_ref[0, :, 128:256] = jnp.zeros((256, 128), BF16)
        v_ref[3, :, 0:128] = jnp.zeros((256, 128), BF16)
        for i in range(3):
            t = tap(k, i, 64)
            f = stack_out(t)
            w_ref[i, 0:128, :] = f
            w_ref[i + 1, 128:256, :] = f
            b = stack_in(t)
            v_ref[2 - i, :, 0:128] = b
            v_ref[3 - i, :, 128:256] = b

    def two(k):
        z = jnp.zeros_like(k)
        return jnp.concatenate([jnp.concatenate([k, z], axis=1), jnp.concatenate([z, k], axis=1)], axis=0)

    r_eo = 64 // dp

    def first_weights():
        k = across("ef")
        for i in range(3):
            w_ef[i] = stack_in(tap(k, i, 256))
        rows = [bias_rows(col[0].astype(F32), 64 // dp) for col in blocks("bias")]
        for n, k in enumerate((0, 1, 2, 4, 5, 6, 3, 7)):
            v = jnp.concatenate([r[k] for r in rows], axis=1)
            v = jnp.concatenate([v, v], axis=1)
            if n < 6:
                bias[n, :, 0:128] = v
            else:
                bias[n] = v * (1.0 / 64.0)
        quad_weights(across("es"), w_es, v_es)

    def second_weights():
        quad_weights(across("et"), w_et, v_et)
        w_eo[...] = two(jnp.concatenate([
            jnp.concatenate([blk.astype(F32)[0:r_eo] for blk in col], axis=1) for col in blocks("eo")], axis=0).astype(BF16))
        w_df[...] = two(across("df"))

    def third_weights():
        quad_weights(across("ds"), w_ds, v_ds)
        quad_weights(across("dt"), w_dt, v_dt)
        quarter = [across(k) for k in range(4)]
        k = jnp.concatenate([quarter[k][16 * b:16 * b + 16] for b in range(4) for k in range(4)], axis=0)
        for i in range(3):
            w_do[i] = stack_out(tap(k, i, 64))

    def to_pairs(v, slot):
        stage[slot, 0] = v[:, :128]
        stage[slot, 1] = v[:, 128:]
        return [jnp.concatenate([stage[slot, h, pl.ds(2 * t + e, 8, stride=16), :] for t in range(8)], axis=0)
                for e in range(2) for h in range(2)]

    def to_natural(v, slot):
        for e in range(2):
            for h in range(2):
                for t in range(8):
                    stage[slot, h, pl.ds(2 * t + e, 8, stride=16), :] = v[8 * t:8 * t + 8, e * 256 + h * 128:e * 256 + h * 128 + 128]
        return stage[slot, 0], stage[slot, 1]

    def source_rows(k):
        def body(r):
            p = 8 * k + r
            v = images[p].astype(F32)
            slot = p % 4 if isinstance(p, int) else lax.rem(p, 4)
            for q, x in enumerate(to_pairs(v, slot)):
                ln = slice(q * 128, q * 128 + 128)
                act, slope = silu_parts(x)
                src[p, :, ln] = x.astype(BF16)
                act0[p + 1, :, ln] = act.astype(BF16)
                sl_src[p, :, ln] = slope
        loop(8, body, U['B'])

    def hidden(pre, b, slope_ref, row):
        act, slope = silu_parts(pre + bias[b, :, 0:128])
        slope_ref[row] = slope
        return act

    def enc_first():
        n = U['nC']

        def body(c):
            p = c * n
            acc = 0.0
            for i in range(3):
                acc = acc + dot_t(act0[pl.ds(p + i, n)].reshape(n * 64, 512), w_ef[i])
            for r, a in enumerate(rows_of(acc, n)):
                put_pair(z1, p + r + 1, hidden(a[:, :128] + folded(a[None, :, 128:])[0], 0, s1, p + r))
        loop(32 // n, body, U['C'])

    def quad_conv(zin, w, b, slope_ref, zout, pair=True):
        n = U['nQ']

        def body(c):
            acc = 0.0
            for d in range(4):
                acc = acc + dot_t(quad_rows(zin, c * n, n, d), w[d])
            for r, a in enumerate(rows_of(acc, n)):
                for e in range(2):
                    row = (c * n + r) * 2 + e
                    act = hidden(a[:, 128 * e:128 * e + 128], b, slope_ref, row)
                    if pair:
                        put_pair(zout, row + 1, act)
                    else:
                        zout[row] = act.astype(BF16)
        loop(16 // n, body, U['Q'])

    def middle_rows():
        n = U['nF']

        def body(c):
            p = c * n
            br = dot(a3[pl.ds(p, n)].reshape(n * 64, 128), w_eo[...])
            for r, a in enumerate(rows_of(br, n)):
                for q in range(4):
                    ln = slice(128 * q, 128 * q + 128)
                    m = src[p + r, :, ln].astype(F32) + (a[:, ln] * (1.0 / 64.0) + bias[6, :, ln])
                    act, slope = silu_parts(m)
                    mid[p + r, :, ln] = m
                    sl_mid[p + r, :, ln] = slope
                    d0[p + r, :, ln] = act.astype(BF16)
            pre = dot_t(d0[pl.ds(p, n)].reshape(n * 64, 512), w_df[...])
            for r, a in enumerate(rows_of(pre, n)):
                put_pair(y1, p + r + 1, hidden(a, 3, t1, p + r))
        loop(32 // n, body, U['F'])

    def result_rows():
        mk = mask[...].astype(F32)
        tall = jnp.sum(mk[:, 0:1])
        broad = jnp.sum(mk[0:1, :])
        sub = lax.broadcasted_iota(jnp.int32, (64, 128), 0)
        column = lax.rem(sub, 8) * 16 + 2 * (sub // 8)
        wi = broad.astype(jnp.int32)
        hi = tall.astype(jnp.int32)
        col_mask = [jnp.where(column + e < wi, 1.0, 0.0) for e in range(2)]
        n = U['nJ']

        def body(c):
            p = c * n
            acc = 0.0
            for i in range(3):
                acc = acc + dot_t(y3[pl.ds(p + i, n)].reshape(n * 64, 256), w_do[i])
            acc = acc.reshape(n, 64, 512)
            for r in range(n):
                m = mid[p + r]
                res = m + (acc[r] * (1.0 / 64.0) + bias[7])
                src[p + r] = res.astype(BF16)
                t = to_pairs(targets[p + r].astype(F32), r % 4)
                row_on = jnp.where(p + r < hi, 1.0, 0.0)
                for q in range(4):
                    ln = slice(q * 128, q * 128 + 128)
                    diff = res[:, ln] - t[q]
                    g = diff * (col_mask[q // 2] * row_on)
                    mid[p + r, :, ln] = g
                    eacc[...] += part_sum(g * diff)
                    g = g * (1.0 / 64.0)
                    g4[p + r + 1, :, ln] = g.astype(BF16)
                    bacc[7, :, ln] += part_sum(g)
        loop(32 // n, body, U['J'])
        return tall * broad

    def decoded_rows(k):
        def body(r):
            p = 8 * k + r
            a, b = to_natural(src[p].astype(F32), p % 4 if isinstance(p, int) else lax.rem(p, 4))
            decoded[p, :, 0:128] = a.astype(BF16)
            decoded[p, :, 128:256] = b.astype(BF16)
        loop(8, body, U['B'])
        return near(decoded.at[pl.ds(8 * k, 8)], decoded_h.at[pl.ds(8 * k, 8)], io_sem.at[2 + k])

    def back(x, slope_ref, row, b):
        g = x * slope_ref[row]
        bacc[b, :, 0:128] += part_sum(g)
        return g

    def dec_last_back():
        n = U['nC']

        def body(c):
            p = c * n
            acc = 0.0
            for i in range(3):
                acc = acc + dot(g4[pl.ds(p + i, n)].reshape(n * 64, 512), w_do[2 - i])
            for r, a in enumerate(rows_of(acc, n)):
                put_pair(zg, p + r + 1, back(a[:, :128] + folded(a[None, :, 128:])[0], t3, p + r, 5))
        loop(32 // n, body, U['K'])

    M = [3, 0, 1, 2]

    def dec_last_weights():
        gv = g4[pl.ds(1, 32)].reshape(2048, 512)
        cols = []
        for i in range(3):
            t = dot_p(gv, y3[pl.ds(i, 32)].reshape(2048, 256))
            for j in range(3):
                a, b = M[j] * 64, M[j + 1] * 64
                cols.append(t[0:256, a:a + 64] + t[256:512, b:b + 64])
        k_do = jnp.concatenate(cols, axis=1).astype(BF16)
        for a in range(dp):
            n = 576 // dp
            v = k_do[:, n * a:n * a + n]
            for b in range(4):
                for k in range(4):
                    at = spots[k][1]
                    r = 64 * b + 16 * k
                    part[2][a // 2, a % 2, b // 2, b % 2, :, at:at + n] = v[r:r + 16]

    def deal(name, k):
        g, at, n = spots[name]
        k = k.astype(BF16)
        for a in range(dp):
            v = k[:, n * a:n * a + n]
            for b in range(4):
                part[g][a // 2, a % 2, b // 2, b % 2, :, at:at + n] = v[16 * b:16 * b + 16]

    def quad_wgrad(z, g_ref, name):
        gq = jnp.concatenate([
            jnp.concatenate([g_ref[2 * r + 1, :, 0:128] for r in range(16)], axis=0),
            jnp.concatenate([g_ref[2 * r + 2, :, 0:128] for r in range(16)], axis=0)], axis=1)
        t = [dot_p(gq, quad_rows(z, 0, 16, d)) for d in range(4)]
        cols = []
        for i in range(3):
            s = t[i][0:128] + t[i + 1][128:256]
            for j in range(3):
                a, b = M[j] * 64, M[j + 1] * 64
                cols.append(s[0:64, a:a + 64] + s[64:128, b:b + 64])
        deal(name, jnp.concatenate(cols, axis=1))

    def quad_back(zin, v, slope_ref, b, zout):
        n = U['nQ']

        def body(c):
            acc = 0.0
            for d in range(4):
                acc = acc + dot(quad_rows(zin, c * n, n, d), v[d])
            for r, a in enumerate(rows_of(acc, n)):
                for e in range(2):
                    row = (c * n + r) * 2 + e
                    put_pair(zout, row + 1, back(a[:, 128 * e:128 * e + 128], slope_ref, row, b))
        loop(16 // n, body, U['Q'])

    def dec_first_weights():
        t = dot_p(zg[pl.ds(1, 32), :, 0:128].reshape(2048, 128), d0[...].reshape(2048, 512))
        deal("df", t[0:64, 0:256] + t[64:128, 256:512])

    def middle_back():
        n = U['nF']

        def body(c):
            p = c * n
            bk = dot(zg[pl.ds(p + 1, n), :, 0:128].reshape(n * 64, 128), w_df[...])
            for r, a in enumerate(rows_of(bk, n)):
                for q in range(4):
                    ln = slice(128 * q, 128 * q + 128)
                    gm = mid[p + r, :, ln] + sl_mid[p + r, :, ln] * a[:, ln]
                    mid[p + r, :, ln] = gm
                    g = gm * (1.0 / 64.0)
                    bacc[6, :, ln] += part_sum(g)
                    h4[p + r, :, ln] = g.astype(BF16)
            x = dot_t(h4[pl.ds(p, n)].reshape(n * 64, 512), w_eo[...])
            for r, a in enumerate(rows_of(x, n)):
                put_pair(zh, p + r + 1, back(a, s3, p + r, 2))
        loop(32 // n, body, U['F'])

    def enc_last_weights():
        t = dot_p(a3[...].reshape(2048, 128), h4[...].reshape(2048, 512))
        k = t[0:64, 0:256] + t[64:128, 256:512]
        g, at, n = spots["eo"]
        for a in range(dp):
            for b in range(4):
                v = eo_block(k[a * r_eo:a * r_eo + r_eo, 64 * b:64 * b + 64])
                part[g][a // 2, a % 2, b // 2, b % 2, :, at:at + n] = v.astype(BF16)

    def enc_first_weights():
        gv = zh[pl.ds(1, 32)].reshape(2048, 256)
        cols = []
        for i in range(3):
            t = dot_p(gv, act0[pl.ds(i, 32)].reshape(2048, 512))
            cols.append(t[64:128, 0:256] + t[128:192, 256:512])
            cols.append(t[0:64, 0:256] + t[64:128, 256:512])
            cols.append(t[192:256, 0:256] + t[0:64, 256:512])
        deal("ef", jnp.concatenate(cols, axis=1))

    def deal_biases():
        sums = []
        for n in (0, 1, 2, 6, 3, 4, 5, 7):
            v = jnp.sum(bacc[n], axis=0, keepdims=True)
            sums.append(v[:, 0:256] + v[:, 256:512] if n >= 6 else v[:, 0:64] + v[:, 64:128])
        g, at, n = spots["bias"]
        for a in range(dp):
            v = bias_block([q[:, a * (q.shape[1] // dp):(a + 1) * (q.shape[1] // dp)] for q in sums]).astype(BF16)
            for b in range(4):
                part[g][a // 2, a % 2, b // 2, b % 2, :, at:at + n] = v

    def source_grad(k):
        n = U['nG']

        def body(c):
            p = 8 * k + c * n
            acc = 0.0
            for i in range(3):
                acc = acc + dot(zh[pl.ds(p + i, n)].reshape(n * 64, 256), w_ef[2 - i])
            acc = acc.reshape(n, 64, 512)
            for r in range(n):
                g = mid[p + r] + sl_src[p + r] * acc[r]
                a, b = to_natural(g, r % 4)
                images_grad[p + r, :, 0:128] = a.astype(BF16)
                images_grad[p + r, :, 128:256] = b.astype(BF16)
        loop(8 // n, body, U['Qr'])

    def source_grad_out(k):
        return near(images_grad.at[pl.ds(8 * k, 8)], images_grad_h.at[pl.ds(8 * k, 8)], image_sem.at[k])

    run = lambda name, f, *args: f(*args)
    for k in range(4):
        image_copies[k].wait()
        run('src%d' % k, source_rows, k)
    g1.square_one()
    g0.cores()
    g2.along_z()
    g0.finish()
    g1.square_two()
    run('w0', first_weights)
    run('enc1', enc_first)
    g1.cores()
    g2.square_one()
    run('enc2', quad_conv, z1, w_es, 1, s2, z2)
    g1.finish()
    run('w1', second_weights)
    g2.square_two()
    run('enc3', quad_conv, z2, w_et, 2, s3, a3, False)
    g2.cores()
    run('middle', middle_rows)
    g2.finish()
    run('w2', third_weights)
    run('dec2', quad_conv, y1, w_ds, 4, t2, y2)
    run('dec3', quad_conv, y2, w_dt, 5, t3, y3)
    mask_copy.wait()
    target_copy.wait()
    pixels = run('result', result_rows)
    loss[0] = 0.5 * jnp.sum(eacc[...]) / (pixels * 256.0)
    run('dec4b', dec_last_back)
    run('dec4w', dec_last_weights)
    run('dec3b', quad_back, zg, v_dt, t2, 4, zh)
    run('dec3w', quad_wgrad, y2, zg, "dt")
    run('dec2b', quad_back, zh, v_ds, t1, 3, zg)
    run('dec2w', quad_wgrad, y1, zh, "ds")
    r2 = Scatter(me, part[2], bufs2, *pairs[6:8])
    r2.cores()
    run('dec1w', dec_first_weights)
    run('midb', middle_back)
    r2.square_one()
    run('enc4w', enc_last_weights)
    run('enc3w', quad_wgrad, z2, zh, "et")
    r1 = Scatter(me, part[1], bufs1, *pairs[8:10])
    r1.cores()
    run('enc3b', quad_back, zh, v_et, s2, 1, zg)
    r2.square_two()
    run('enc2w', quad_wgrad, z1, zg, "es")
    run('enc2b', quad_back, zg, v_es, s1, 0, zh)
    run('bias', deal_biases)
    r1.square_one()
    run('enc1w', enc_first_weights)
    r0 = DirectScatter(me, part[0], bufs0, *pairs[10:12])
    r0.cores()
    r2.along_z()
    out_copies = []
    for k in range(2):
        out_copies.append(run('out%d' % k, decoded_rows, k))
    r1.square_two()
    run('grad0', source_grad, 0)
    out_copies.append(source_grad_out(0))
    r0.chips()
    for k in range(1, 4):
        run('grad%d' % k, source_grad, k)
        out_copies.append(source_grad_out(k))
    r1.along_z()
    for k in range(2, 4):
        out_copies.append(run('out%d' % k, decoded_rows, k))
    r2.finish(tot2)
    r1.finish(tot1)
    r0.finish(tot0)
    wait_all(out_copies)


def last_kernel(decoded_i, images_grad_i, loss_i, *refs):
    tots_i, (decoded, images_grad, loss), refs = refs[:3], refs[3:6], refs[6:]
    outs_h, refs = refs[:16], refs[16:]
    outs, tots, hold, sem, tot_sem, out_sem = refs[:16], refs[16:19], *refs[19:]
    dp = 64 // outs[3].shape[0]
    small = [pltpu.make_async_copy(p, q, tot_sem.at[k]) for k, (p, q) in enumerate(zip(tots_i, tots))]
    pairs = [(p, q, n * 4 + k, pl.ds(8 * k, 8)) for k in range(4) for n, (p, q) in enumerate(((decoded_i, decoded), (images_grad_i, images_grad)))]
    ins = [pltpu.make_async_copy(p.at[rows], hold.at[k], sem.at[k]) for p, q, k, rows in pairs]
    backs = [pltpu.make_async_copy(hold.at[k], q.at[rows], sem.at[8 + k]) for p, q, k, rows in pairs]
    for cp in small + ins:
        cp.start()
    loss[0] = loss_i[0]
    wait_all(small)
    spots, _ = places(dp)

    def piece(name):
        g, at, n = spots[name]
        return tots[g][:, at:at + n]
    for k, name in enumerate(("ef", "es", "et", None, "df", "ds", "dt")):
        if name:
            outs[k][...] = piece(name)
    outs[3][...] = piece("eo")[0:64 // dp]
    for k in range(4):
        outs[7][16 * k:16 * k + 16] = piece(k)
    for ref, v in zip(outs[8:], bias_rows(piece("bias"), 64 // dp)):
        ref[...] = v
    last = [pltpu.make_async_copy(p, q, out_sem.at[k]) for k, (p, q) in enumerate(zip(outs, outs_h))]
    for cp in last:
        cp.start()
    for p, q in zip(ins, backs):
        p.wait()
        q.start()
    wait_all(last + backs)


U = dict(B=4, nC=32, C=1, K=1, nQ=16, Q=1, nF=16, F=1, nJ=16, J=1, nG=8, Qr=1)


def per_device(images, targets, pixel_mask, ef, es, et, eo, eba, ebb, ebc, ebd, df, ds, dt, do, dba, dbb, dbc, dbd):
    dp = lax.axis_size("dp")
    nz = dp // 2
    h = nz // 2
    widths = places(dp)[1]
    chips = len(chip_steps(nz))
    vm = pl.BlockSpec(memory_space=pltpu.VMEM)
    far = pl.BlockSpec(memory_space=pl.ANY)
    smem = pl.BlockSpec(memory_space=pltpu.SMEM)
    sem = pltpu.SemaphoreType.DMA
    V = lambda shape, dt: pltpu.VMEM(shape, dt)
    S = jax.ShapeDtypeStruct
    args = [images[0], targets[0], pixel_mask[0], ef.T, es.T, et.T, eo, df.T, ds.T, dt.T, do.T]
    args += [b.reshape(1, -1) for b in (eba, ebb, ebc, ebd, dba, dbb, dbc, dbd)]
    comm = lambda wide: [
        V((nz, 2, 2, 16, wide), BF16), V((nz, 2, 2, 16, wide), BF16), V((h, 2, 16, wide), BF16), V((nz - h, 2, 16, wide), BF16),
        V((h, 2, 16, wide), BF16), V((nz - h, 2, 16, wide), BF16), V((nz, 16, wide), BF16), V((nz, 16, wide), BF16),
        V((nz, 16, wide), BF16)]
    direct = [V((nz, 2, 2, 16, widths[0]), BF16)] * 2 + [V((chips, 16, widths[0]), BF16)]
    big = S((32, 128, 256), BF16)
    tots = [S((16, w), F32) for w in widths]
    decoded, images_grad, loss, *kept = pl.pallas_call(
        functools.partial(main_kernel, U),
        out_shape=[big, big, S((1,), F32), *tots],
        in_specs=[far] * 19, out_specs=[far, far, smem, vm, vm, vm],
        scratch_shapes=[V(a.shape, a.dtype) for a in args] + [
            V((32, 64, 512), BF16), V((34, 64, 512), BF16), V((32, 64, 512), F32),
            V((34, 64, 256), BF16), V((34, 64, 256), BF16), V((32, 64, 128), BF16),
            V((34, 64, 256), BF16), V((34, 64, 256), BF16), V((34, 64, 256), BF16)] + [V((32, 64, 128), F32)] * 6 + [
            V((32, 64, 512), F32), V((32, 64, 512), F32), V((32, 64, 512), BF16),
            V((34, 64, 512), BF16), V((32, 64, 512), BF16), V((34, 64, 256), BF16), V((34, 64, 256), BF16),
            V((4, 2, 128, 128), F32),
            V((3, 256, 512), BF16)] + [V((4, 256, 256), BF16)] * 8 + [
            V((3, 512, 256), BF16), V((128, 512), BF16), V((128, 512), BF16),
            V((8, 1, 512), F32), V((8, 8, 512), F32), V((8, 128), F32)]
        + [V((nz, 2, 2, 2, 16, w), BF16) for w in widths] * 2 + direct + comm(widths[1]) + comm(widths[2])
        + [sem((16,)), sem((4,)), sem((6,))] + [sem((chips + nz,))] * 2 + [sem((nz + 4,))] * 8 + [sem((chips + 1,))] * 2,
        compiler_params=pltpu.CompilerParams(collective_id=0, has_side_effects=True, vmem_limit_bytes=63 * 2**20),
    )(*args)
    f = lambda *s: S(s, F32)
    grads = [f(16, 2304 // dp), f(16, 576 // dp), f(16, 576 // dp), f(64 // dp, 64), f(16, 256 // dp),
             f(16, 576 // dp), f(16, 576 // dp), f(64, 576 // dp)] + [f(1, s // dp) for s in (64, 64, 64, 256) * 2]
    outs = pl.pallas_call(
        last_kernel,
        out_shape=[big, big, S((1,), F32)] + grads,
        in_specs=[far, far, smem, far, far, far], out_specs=[far, far, smem] + [far] * 16,
        scratch_shapes=[V(g.shape, F32) for g in grads + tots] + [V((8, 8, 128, 256), BF16), sem((16,)), sem((3,)), sem((16,))],
        compiler_params=pltpu.CompilerParams(vmem_limit_bytes=60 * 2**20),
    )(decoded, images_grad, loss, *kept)
    decoded, images_grad, loss, g_ef, g_es, g_et, g_eo, g_df, g_ds, g_dt, g_do = outs[:11]
    bs = [b.reshape(-1) for b in outs[11:]]
    return (decoded[None], images_grad[None], loss, g_ef.T, g_es.T, g_et.T, g_eo, *bs[:4],
            g_df.T, g_ds.T, g_dt.T, g_do.T, *bs[4:])


def solution(mesh):
    img, w, b = P(("dp", "fsdp"), None, None, None), P("dp", "fsdp"), P("dp")
    placed = (img, img, P(("dp", "fsdp"), None, None)) + (w,) * 4 + (b,) * 4 + (w,) * 4 + (b,) * 4
    return jax.shard_map(
        per_device, mesh=mesh, in_specs=placed,
        out_specs=(img, img, P(("dp", "fsdp"))) + (w,) * 4 + (b,) * 4 + (w,) * 4 + (b,) * 4,
        check_vma=False)
```

time: 80.5 us -> 69.3 us (0.86)
  Pallas kernels: 79.4 us -> 68.2 us
    pallas_call x1, Pallas kernels: 73.7 us -> 62.6 us  [per_device(): pl.pallas_call(functools.partial(main_kernel, U), out_shape=[big, big, S(...]
where the time goes in v1:
time: 69.3 us; the launch traced here: 69 us
  Pallas kernels  68.2 us (98%)
  between operations  0.85 us (1%)
    pallas_call x1, Pallas kernels, per_device(): pl.pallas_call(functools.partial(main_kernel, U), out_shape=[big, big, S(...  62.6 us
    pallas_call x1, Pallas kernels, per_device(): pl.pallas_call(last_kernel, out_shape=[big, big, S((1,), F32)] + grads, i...  5.63 us

profile of v1, /device:TPU:0, one launch (start us, length us, event | category | flops | bytes accessed | tf_op | source)
XLA Modules:
  0.0 69.0 jit_solution(92082240151191000)
XLA Ops:
  0.7 62.6 %shard_map.330 = (bf16[32,128,256]{2,1,0:T(8,128)(2,1)}, bf16[32,128,256]{2,1,0:T(8,128)(2,1)}, f32[1]{0:T(128)}, f32[16,384]{1,0:T(8,128)}, f32[16,256]{1,0:T(8,128)}, /*index=5*/f32[16,512]{1,0:T(8,128)}) custom-call(bf16[32,128,256]{2,1,0:T(8,128)(2,1)} %bitcast.35, bf16[32,128,256]{2,1,0:T(8,128)(2,1)} %bitcast.36, s32[32,128]{1,0:T(8,128)} %bitcast.37, ...), custom_call_target="tpu_custom_call" | custom-call | tf_op jit(solution)/shard_map/pallas_call | solution.py:845
  63.2 5.6 %shard_map.331 = (bf16[32,128,256]{2,1,0:T(8,128)(2,1)}, bf16[32,128,256]{2,1,0:T(8,128)(2,1)}, f32[1]{0:T(128)}, f32[16,288]{1,0:T(8,128)}, f32[16,72]{1,0:T(8,...) custom-call(bf16[32,128,256]{2,1,0:T(8,128)(2,1)} %get-tuple-element, ...), custom_call_target="tpu_custom_call" | custom-call | tf_op jit(solution)/shard_map/pallas_call | solution.py:866

commit v2 on v1

--- a/solution.py
+++ b/solution.py
@@ -237,13 +237,15 @@
         self.in1, self.s1, self.in2 = bufs
         self.nz = part.shape[0]
         self.steps = chip_steps(self.nz)
+        self.fly = []
 
     def copy(self, src, dst, k, to):
         return far_copy(src, dst, self.send.at[k], self.recv.at[k], device(*to))
 
-    def cores(self):
+    def cores(self, k, lo, hi):
         z, y, x, c = self.me
-        self.fly = [self.copy(self.part.at[:, :, :, 1 - c], self.in1, len(self.steps), (z, y, x, 1 - c))]
+        rows = pl.ds(lo, hi - lo)
+        self.fly.append(self.copy(self.part.at[rows, :, :, 1 - c], self.in1.at[rows], len(self.steps) + k, (z, y, x, 1 - c)))
 
     def chips(self):
         z, y, x, c = self.me
@@ -277,62 +279,6 @@
     return (p.astype(F32) + q.astype(F32)).astype(BF16)
 
 
-class Scatter:
-    def __init__(self, me, part, bufs, send, recv):
-        self.me, self.part, self.send, self.recv = me, part, send, recv
-        self.in1, self.s1, self.in2a, self.in2b, self.s2a, self.s2b, self.in3, self.s3, self.in4 = bufs
-        self.nz = part.shape[0]
-        self.h = self.nz // 2
-
-    def copy(self, src, dst, k, to):
-        return far_copy(src, dst, self.send.at[k], self.recv.at[k], device(*to))
-
-    def cores(self):
-        z, y, x, c = self.me
-        self.fly = [self.copy(self.part.at[:, :, :, 1 - c], self.in1, 0, (z, y, x, 1 - c))]
-
-    def square_one(self):
-        z, y, x, c = self.me
-        h, n = self.h, self.nz - self.h
-        wait_all(self.fly)
-        for k in range(self.nz):
-            self.s1[k] = add16(self.part[k, :, :, c], self.in1[k])
-        self.fly = [self.copy(self.s1.at[pl.ds(0, h), :, 1 - x], self.in2a, 1, (z, y, 1 - x, c)),
-                    self.copy(self.s1.at[pl.ds(h, n), 1 - y], self.in2b, 2, (z, 1 - y, x, c))]
-
-    def square_two(self):
-        z, y, x, c = self.me
-        h, n = self.h, self.nz - self.h
-        wait_all(self.fly)
-        for k in range(h):
-            self.s2a[k] = add16(self.s1[k, :, x], self.in2a[k])
-        for k in range(n):
-            self.s2b[k] = add16(self.s1[h + k, y], self.in2b[k])
-        self.fly = [self.copy(self.s2a.at[:, 1 - y], self.in3.at[pl.ds(0, h)], 3, (z, 1 - y, x, c)),
-                    self.copy(self.s2b.at[:, 1 - x], self.in3.at[pl.ds(h, n)], 4, (z, y, 1 - x, c))]
-
-    def along_z(self):
-        z, y, x, c = self.me
-        h, n = self.h, self.nz - self.h
-        wait_all(self.fly)
-        for k in range(h):
-            self.s3[k] = add16(self.s2a[k, y], self.in3[k])
-        for k in range(n):
-            self.s3[h + k] = add16(self.s2b[k, x], self.in3[h + k])
-        self.fly = []
-        for k in range(1, self.nz):
-            other = lax.rem(z + k, self.nz)
-            self.fly.append(self.copy(self.s3.at[other], self.in4.at[k], 4 + k, (other, y, x, c)))
-
-    def finish(self, out):
-        z = self.me[0]
-        wait_all(self.fly)
-        total = self.s3[z].astype(F32)
-        for k in range(1, self.nz):
-            total = total + self.in4[k].astype(F32)
-        out[...] = total
-
-
 def main_kernel(U, *refs):
     (images_h, targets_h, mask_h, ef_h, es_h, et_h, eo_h, df_h, ds_h, dt_h, do_h, *rest) = refs
     biases_h, rest = rest[:8], rest[8:]
@@ -342,10 +288,10 @@
     decoded, images_grad = images, targets
     (src, act0, sl_src, z1, z2, a3, y1, y2, y3, s1, s2, s3, t1, t2, t3,
      mid, sl_mid, d0, g4, h4, zg, zh, stage,
-     w_ef, w_es, w_et, v_es, v_et, w_ds, w_dt, v_ds, v_dt, w_do, w_eo, w_df, bias, bacc, eacc,
+     w_ef, w_es, w_et, v_es, v_et, w_ds, w_dt, v_ds, v_dt, w_do, w_eo, w_df, bias, bacc, eacc, tp,
      *rest) = rest
     whole, part, rest = rest[:3], rest[3:6], rest[6:]
-    bufs0, bufs1, bufs2, rest = rest[:3], rest[3:12], rest[12:21], rest[21:]
+    bufs0, bufs1, bufs2, rest = rest[:3], rest[3:6], rest[6:9], rest[9:]
     shard_sem, image_sem, io_sem, *pairs = rest
 
     nz = whole[0].shape[0]
@@ -353,6 +299,11 @@
     spots, widths = places(dp)
     me = where_am_i()
     z, y, x, c = me
+
+    barrier = pltpu.get_barrier_semaphore()
+    others = [device(*other_chip(me, step, nz)) for step in chip_steps(nz)] + [device(z, y, x, 1 - c)]
+    for d in others:
+        pl.semaphore_signal(barrier, inc=1, device_id=d, device_id_type=MESH)
 
     def near(src, dst, sem):
         cp = pltpu.make_async_copy(src, dst, sem)
@@ -365,13 +316,9 @@
     target_copy = near(targets_h, targets, io_sem.at[0])
     mask_copy = near(mask_h, mask, io_sem.at[1])
 
-    barrier = pltpu.get_barrier_semaphore()
-    others = [device(*other_chip(me, step, nz)) for step in chip_steps(nz)] + [device(z, y, x, 1 - c)]
-    for d in others:
-        pl.semaphore_signal(barrier, inc=1, device_id=d, device_id_type=MESH)
     g0 = DirectGather(me, whole[0], *pairs[0:2])
     g1 = Gather(me, whole[1], *pairs[2:4])
-    g2 = Gather(me, whole[2], *pairs[4:6])
+    g2 = DirectGather(me, whole[2], *pairs[4:6])
     wait_all(shard_copies)
     bias_part = bias_block([b[...].astype(F32) for b in biases_s]).astype(BF16)
     whole[0][z, y, x, c] = lanes_to([ef_s[...], es_s[...], bias_part], widths[0])
@@ -471,6 +418,13 @@
                 sl_src[p, :, ln] = slope
         loop(8, body, U['B'])
 
+    def target_rows():
+        def body(p):
+            slot = p % 4 if isinstance(p, int) else lax.rem(p, 4)
+            for q, t in enumerate(to_pairs(targets[p].astype(F32), slot)):
+                tp[p, :, q * 128:q * 128 + 128] = t.astype(BF16)
+        loop(32, body, U['B'])
+
     def hidden(pre, b, slope_ref, row):
         act, slope = silu_parts(pre + bias[b, :, 0:128])
         slope_ref[row] = slope
@@ -505,11 +459,11 @@
                         zout[row] = act.astype(BF16)
         loop(16 // n, body, U['Q'])
 
-    def middle_rows():
+    def middle_rows(k):
         n = U['nF']
 
         def body(c):
-            p = c * n
+            p = 16 * k + c * n
             br = dot(a3[pl.ds(p, n)].reshape(n * 64, 128), w_eo[...])
             for r, a in enumerate(rows_of(br, n)):
                 for q in range(4):
@@ -522,7 +476,7 @@
             pre = dot_t(d0[pl.ds(p, n)].reshape(n * 64, 512), w_df[...])
             for r, a in enumerate(rows_of(pre, n)):
                 put_pair(y1, p + r + 1, hidden(a, 3, t1, p + r))
-        loop(32 // n, body, U['F'])
+        loop(16 // n, body, U['F'])
 
     def result_rows():
         mk = mask[...].astype(F32)
@@ -545,11 +499,10 @@
                 m = mid[p + r]
                 res = m + (acc[r] * (1.0 / 64.0) + bias[7])
                 src[p + r] = res.astype(BF16)
-                t = to_pairs(targets[p + r].astype(F32), r % 4)
                 row_on = jnp.where(p + r < hi, 1.0, 0.0)
                 for q in range(4):
                     ln = slice(q * 128, q * 128 + 128)
-                    diff = res[:, ln] - t[q]
+                    diff = res[:, ln] - tp[p + r, :, ln].astype(F32)
                     g = diff * (col_mask[q // 2] * row_on)
                     mid[p + r, :, ln] = g
                     eacc[...] += part_sum(g * diff)
@@ -671,15 +624,24 @@
                 v = eo_block(k[a * r_eo:a * r_eo + r_eo, 64 * b:64 * b + 64])
                 part[g][a // 2, a % 2, b // 2, b % 2, :, at:at + n] = v.astype(BF16)
 
-    def enc_first_weights():
+    def enc_first_weights(r0):
         gv = zh[pl.ds(1, 32)].reshape(2048, 256)
-        cols = []
+        g, at, n = spots["ef"]
+        cols, done, sent = [], 0, 0
         for i in range(3):
             t = dot_p(gv, act0[pl.ds(i, 32)].reshape(2048, 512))
-            cols.append(t[64:128, 0:256] + t[128:192, 256:512])
-            cols.append(t[0:64, 0:256] + t[64:128, 256:512])
-            cols.append(t[192:256, 0:256] + t[0:64, 256:512])
-        deal("ef", jnp.concatenate(cols, axis=1))
+            cols.append((t[64:128, 0:256] + t[128:192, 256:512]).astype(BF16))
+            cols.append((t[0:64, 0:256] + t[64:128, 256:512]).astype(BF16))
+            cols.append((t[192:256, 0:256] + t[0:64, 256:512]).astype(BF16))
+            k = jnp.concatenate(cols, axis=1)
+            ready = dp * (i + 1) // 3
+            for a in range(done, ready):
+                v = k[:, n * a:n * a + n]
+                for b in range(4):
+                    part[g][a // 2, a % 2, b // 2, b % 2, :, at:at + n] = v[16 * b:16 * b + 16]
+            done = ready
+            r0.cores(i, sent, done // 2)
+            sent = done // 2
 
     def deal_biases():
         sums = []
@@ -715,28 +677,28 @@
     for k in range(4):
         image_copies[k].wait()
         run('src%d' % k, source_rows, k)
+    target_copy.wait()
+    run('targets', target_rows)
     g1.square_one()
     g0.cores()
-    g2.along_z()
+    g2.chips()
     g0.finish()
     g1.square_two()
     run('w0', first_weights)
     run('enc1', enc_first)
     g1.cores()
-    g2.square_one()
     run('enc2', quad_conv, z1, w_es, 1, s2, z2)
     g1.finish()
     run('w1', second_weights)
-    g2.square_two()
     run('enc3', quad_conv, z2, w_et, 2, s3, a3, False)
+    run('middle', middle_rows, 0)
     g2.cores()
-    run('middle', middle_rows)
+    run('middle', middle_rows, 1)
     g2.finish()
     run('w2', third_weights)
     run('dec2', quad_conv, y1, w_ds, 4, t2, y2)
     run('dec3', quad_conv, y2, w_dt, 5, t3, y3)
     mask_copy.wait()
-    target_copy.wait()
     pixels = run('result', result_rows)
     loss[0] = 0.5 * jnp.sum(eacc[...]) / (pixels * 256.0)
     run('dec4b', dec_last_back)
@@ -745,36 +707,29 @@
     run('dec3w', quad_wgrad, y2, zg, "dt")
     run('dec2b', quad_back, zh, v_ds, t1, 3, zg)
     run('dec2w', quad_wgrad, y1, zh, "ds")
-    r2 = Scatter(me, part[2], bufs2, *pairs[6:8])
-    r2.cores()
+    r2 = DirectScatter(me, part[2], bufs2, *pairs[6:8])
+    r2.cores(0, 0, nz)
     run('dec1w', dec_first_weights)
     run('midb', middle_back)
-    r2.square_one()
+    r2.chips()
     run('enc4w', enc_last_weights)
     run('enc3w', quad_wgrad, z2, zh, "et")
-    r1 = Scatter(me, part[1], bufs1, *pairs[8:10])
-    r1.cores()
+    r1 = DirectScatter(me, part[1], bufs1, *pairs[8:10])
+    r1.cores(0, 0, nz)
     run('enc3b', quad_back, zh, v_et, s2, 1, zg)
-    r2.square_two()
+    r1.chips()
     run('enc2w', quad_wgrad, z1, zg, "es")
     run('enc2b', quad_back, zg, v_es, s1, 0, zh)
     run('bias', deal_biases)
-    r1.square_one()
-    run('enc1w', enc_first_weights)
     r0 = DirectScatter(me, part[0], bufs0, *pairs[10:12])
-    r0.cores()
-    r2.along_z()
+    run('enc1w', enc_first_weights, r0)
     out_copies = []
     for k in range(2):
         out_copies.append(run('out%d' % k, decoded_rows, k))
-    r1.square_two()
-    run('grad0', source_grad, 0)
-    out_copies.append(source_grad_out(0))
     r0.chips()
-    for k in range(1, 4):
+    for k in range(4):
         run('grad%d' % k, source_grad, k)
         out_copies.append(source_grad_out(k))
-    r1.along_z()
     for k in range(2, 4):
         out_copies.append(run('out%d' % k, decoded_rows, k))
     r2.finish(tot2)
@@ -789,9 +744,9 @@
     outs, tots, hold, sem, tot_sem, out_sem = refs[:16], refs[16:19], *refs[19:]
     dp = 64 // outs[3].shape[0]
     small = [pltpu.make_async_copy(p, q, tot_sem.at[k]) for k, (p, q) in enumerate(zip(tots_i, tots))]
-    pairs = [(p, q, n * 4 + k, pl.ds(8 * k, 8)) for k in range(4) for n, (p, q) in enumerate(((decoded_i, decoded), (images_grad_i, images_grad)))]
+    pairs = [(p, q, n * 2 + k, pl.ds(16 * k, 16)) for k in range(2) for n, (p, q) in enumerate(((decoded_i, decoded), (images_grad_i, images_grad)))]
     ins = [pltpu.make_async_copy(p.at[rows], hold.at[k], sem.at[k]) for p, q, k, rows in pairs]
-    backs = [pltpu.make_async_copy(hold.at[k], q.at[rows], sem.at[8 + k]) for p, q, k, rows in pairs]
+    backs = [pltpu.make_async_copy(hold.at[k], q.at[rows], sem.at[4 + k]) for p, q, k, rows in pairs]
     for cp in small + ins:
         cp.start()
     loss[0] = loss_i[0]
@@ -810,11 +765,11 @@
     for ref, v in zip(outs[8:], bias_rows(piece("bias"), 64 // dp)):
         ref[...] = v
     last = [pltpu.make_async_copy(p, q, out_sem.at[k]) for k, (p, q) in enumerate(zip(outs, outs_h))]
-    for cp in last:
-        cp.start()
     for p, q in zip(ins, backs):
         p.wait()
         q.start()
+    for cp in last:
+        cp.start()
     wait_all(last + backs)
 
 
@@ -824,7 +779,6 @@
 def per_device(images, targets, pixel_mask, ef, es, et, eo, eba, ebb, ebc, ebd, df, ds, dt, do, dba, dbb, dbc, dbd):
     dp = lax.axis_size("dp")
     nz = dp // 2
-    h = nz // 2
     widths = places(dp)[1]
     chips = len(chip_steps(nz))
     vm = pl.BlockSpec(memory_space=pltpu.VMEM)
@@ -835,11 +789,9 @@
     S = jax.ShapeDtypeStruct
     args = [images[0], targets[0], pixel_mask[0], ef.T, es.T, et.T, eo, df.T, ds.T, dt.T, do.T]
     args += [b.reshape(1, -1) for b in (eba, ebb, ebc, ebd, dba, dbb, dbc, dbd)]
-    comm = lambda wide: [
-        V((nz, 2, 2, 16, wide), BF16), V((nz, 2, 2, 16, wide), BF16), V((h, 2, 16, wide), BF16), V((nz - h, 2, 16, wide), BF16),
-        V((h, 2, 16, wide), BF16), V((nz - h, 2, 16, wide), BF16), V((nz, 16, wide), BF16), V((nz, 16, wide), BF16),
-        V((nz, 16, wide), BF16)]
-    direct = [V((nz, 2, 2, 16, widths[0]), BF16)] * 2 + [V((chips, 16, widths[0]), BF16)]
+    sums = []
+    for w in widths:
+        sums += [V((nz, 2, 2, 16, w), BF16)] * 2 + [V((chips, 16, w), BF16)]
     big = S((32, 128, 256), BF16)
     tots = [S((16, w), F32) for w in widths]
     decoded, images_grad, loss, *kept = pl.pallas_call(
@@ -855,9 +807,9 @@
             V((4, 2, 128, 128), F32),
             V((3, 256, 512), BF16)] + [V((4, 256, 256), BF16)] * 8 + [
             V((3, 512, 256), BF16), V((128, 512), BF16), V((128, 512), BF16),
-            V((8, 1, 512), F32), V((8, 8, 512), F32), V((8, 128), F32)]
-        + [V((nz, 2, 2, 2, 16, w), BF16) for w in widths] * 2 + direct + comm(widths[1]) + comm(widths[2])
-        + [sem((16,)), sem((4,)), sem((6,))] + [sem((chips + nz,))] * 2 + [sem((nz + 4,))] * 8 + [sem((chips + 1,))] * 2,
+            V((8, 1, 512), F32), V((8, 8, 512), F32), V((8, 128), F32), V((32, 64, 512), BF16)]
+        + [V((nz, 2, 2, 2, 16, w), BF16) for w in widths] * 2 + sums
+        + [sem((16,)), sem((4,)), sem((6,))] + [sem((chips + nz,))] * 2 + [sem((nz + 4,))] * 2 + [sem((chips + nz,))] * 2 + [sem((chips + 3,))] * 6,
         compiler_params=pltpu.CompilerParams(collective_id=0, has_side_effects=True, vmem_limit_bytes=63 * 2**20),
     )(*args)
     f = lambda *s: S(s, F32)
@@ -867,7 +819,7 @@
         last_kernel,
         out_shape=[big, big, S((1,), F32)] + grads,
         in_specs=[far, far, smem, far, far, far], out_specs=[far, far, smem] + [far] * 16,
-        scratch_shapes=[V(g.shape, F32) for g in grads + tots] + [V((8, 8, 128, 256), BF16), sem((16,)), sem((3,)), sem((16,))],
+        scratch_shapes=[V(g.shape, F32) for g in grads + tots] + [V((4, 16, 128, 256), BF16), sem((8,)), sem((3,)), sem((16,))],
         compiler_params=pltpu.CompilerParams(vmem_limit_bytes=60 * 2**20),
     )(decoded, images_grad, loss, *kept)
     decoded, images_grad, loss, g_ef, g_es, g_et, g_eo, g_df, g_ds, g_dt, g_do = outs[:11]

time: 69.3 us -> 65.7 us (0.948)
  Pallas kernels: 68.2 us -> 64.6 us
    pallas_call x1, Pallas kernels: 62.6 us -> 59.3 us  [per_device(): pl.pallas_call(functools.partial(main_kernel, U), out_shape=[big, big, S(...]
where the time goes in v2:
time: 65.7 us; the launch traced here: 65.4 us
  Pallas kernels  64.6 us (98%)
  between operations  0.85 us (1%)
    pallas_call x1, Pallas kernels, per_device(): pl.pallas_call(functools.partial(main_kernel, U), out_shape=[big, big, S(...  59.3 us
    pallas_call x1, Pallas kernels, per_device(): pl.pallas_call(last_kernel, out_shape=[big, big, S((1,), F32)] + grads, i...  5.28 us

profile of v2, /device:TPU:0, one launch (start us, length us, event | category | flops | bytes accessed | tf_op | source)
XLA Modules:
  0.0 65.4 jit_solution(1293437981851407688)
XLA Ops:
  0.7 59.3 %shard_map.330 = (bf16[32,128,256]{2,1,0:T(8,128)(2,1)}, bf16[32,128,256]{2,1,0:T(8,128)(2,1)}, f32[1]{0:T(128)}, f32[16,384]{1,0:T(8,128)}, f32[16,256]{1,0:T(8,128)}, /*index=5*/f32[16,512]{1,0:T(8,128)}) custom-call(bf16[32,128,256]{2,1,0:T(8,128)(2,1)} %bitcast.35, bf16[32,128,256]{2,1,0:T(8,128)(2,1)} %bitcast.36, s32[32,128]{1,0:T(8,128)} %bitcast.37, ...), custom_call_target="tpu_custom_call" | custom-call | tf_op jit(solution)/shard_map/pallas_call | solution.py:797
  60.0 5.3 %shard_map.331 = (bf16[32,128,256]{2,1,0:T(8,128)(2,1)}, bf16[32,128,256]{2,1,0:T(8,128)(2,1)}, f32[1]{0:T(128)}, f32[16,288]{1,0:T(8,128)}, f32[16,72]{1,0:T(8,...) custom-call(bf16[32,128,256]{2,1,0:T(8,128)(2,1)} %get-tuple-element, ...), custom_call_target="tpu_custom_call" | custom-call | tf_op jit(solution)/shard_map/pallas_call | solution.py:818

commit v3 on v2

--- a/solution.py
+++ b/solution.py
@@ -597,7 +597,7 @@
         deal("df", t[0:64, 0:256] + t[64:128, 256:512])
 
     def middle_back():
-        n = U['nF']
+        n = U['nN']
 
         def body(c):
             p = c * n
@@ -658,7 +658,7 @@
         n = U['nG']
 
         def body(c):
-            p = 8 * k + c * n
+            p = 16 * k + c * n
             acc = 0.0
             for i in range(3):
                 acc = acc + dot(zh[pl.ds(p + i, n)].reshape(n * 64, 256), w_ef[2 - i])
@@ -668,10 +668,10 @@
                 a, b = to_natural(g, r % 4)
                 images_grad[p + r, :, 0:128] = a.astype(BF16)
                 images_grad[p + r, :, 128:256] = b.astype(BF16)
-        loop(8 // n, body, U['Qr'])
+        loop(16 // n, body, U['Qr'])
 
     def source_grad_out(k):
-        return near(images_grad.at[pl.ds(8 * k, 8)], images_grad_h.at[pl.ds(8 * k, 8)], image_sem.at[k])
+        return near(images_grad.at[pl.ds(16 * k, 16)], images_grad_h.at[pl.ds(16 * k, 16)], image_sem.at[k])
 
     run = lambda name, f, *args: f(*args)
     for k in range(4):
@@ -727,7 +727,7 @@
     for k in range(2):
         out_copies.append(run('out%d' % k, decoded_rows, k))
     r0.chips()
-    for k in range(4):
+    for k in range(2):
         run('grad%d' % k, source_grad, k)
         out_copies.append(source_grad_out(k))
     for k in range(2, 4):
@@ -773,7 +773,7 @@
     wait_all(last + backs)
 
 
-U = dict(B=4, nC=32, C=1, K=1, nQ=16, Q=1, nF=16, F=1, nJ=16, J=1, nG=8, Qr=1)
+U = dict(B=4, nC=32, C=1, K=1, nQ=16, Q=1, nF=16, F=1, nJ=32, J=1, nG=16, Qr=1, nN=32)
 
 
 def per_device(images, targets, pixel_mask, ef, es, et, eo, eba, ebb, ebc, ebd, df, ds, dt, do, dba, dbb, dbc, dbd):

time: 65.7 us -> 64.2 us (0.977)
  Pallas kernels: 64.6 us -> 63.1 us
    pallas_call x1, Pallas kernels: 59.3 us -> 57.8 us  [per_device(): pl.pallas_call(functools.partial(main_kernel, U), out_shape=[big, big, S(...]
where the time goes in v3:
time: 64.2 us; the launch traced here: 64 us
  Pallas kernels  63.1 us (98%)
  between operations  0.85 us (1%)
    pallas_call x1, Pallas kernels, per_device(): pl.pallas_call(functools.partial(main_kernel, U), out_shape=[big, big, S(...  57.8 us
    pallas_call x1, Pallas kernels, per_device(): pl.pallas_call(last_kernel, out_shape=[big, big, S((1,), F32)] + grads, i...  5.28 us

profile of v3, /device:TPU:0, one launch (start us, length us, event | category | flops | bytes accessed | tf_op | source)
XLA Modules:
  0.0 64.0 jit_solution(5580421203943316986)
XLA Ops:
  0.7 57.8 %shard_map.330 = (bf16[32,128,256]{2,1,0:T(8,128)(2,1)}, bf16[32,128,256]{2,1,0:T(8,128)(2,1)}, f32[1]{0:T(128)}, f32[16,384]{1,0:T(8,128)}, f32[16,256]{1,0:T(8,128)}, /*index=5*/f32[16,512]{1,0:T(8,128)}) custom-call(bf16[32,128,256]{2,1,0:T(8,128)(2,1)} %bitcast.35, bf16[32,128,256]{2,1,0:T(8,128)(2,1)} %bitcast.36, s32[32,128]{1,0:T(8,128)} %bitcast.37, ...), custom_call_target="tpu_custom_call" | custom-call | tf_op jit(solution)/shard_map/pallas_call | solution.py:797
  58.5 5.3 %shard_map.331 = (bf16[32,128,256]{2,1,0:T(8,128)(2,1)}, bf16[32,128,256]{2,1,0:T(8,128)(2,1)}, f32[1]{0:T(128)}, f32[16,288]{1,0:T(8,128)}, f32[16,72]{1,0:T(8,...) custom-call(bf16[32,128,256]{2,1,0:T(8,128)(2,1)} %get-tuple-element, ...), custom_call_target="tpu_custom_call" | custom-call | tf_op jit(solution)/shard_map/pallas_call | solution.py:818
